TPU v7x, 256 devices: a whole 4x4x8 slice. The times are simulated.
256 devices in a mesh: cache: 32 (over x, z), tensor: 8 (over y, core).
Axes of the slice: x: 4, y: 4, z: 8, core: 2. Of those that a mesh axis runs over, the one named last changes fastest.
Arguments:
- queries: bfloat16 [1024, 32, 8192], P('cache', None, 'tensor'), may hold values from -18 to 18
- prefix_kv: bfloat16 [2, 32, 512, 1024], P(None, 'cache', None, 'tensor'), may hold values from -12 to 12
- suffix_kv: bfloat16 [2, 1024, 32, 1024], P(None, 'cache', None, 'tensor'), may hold values from -12 to 12
- candidate_prefix: int32 [1024, 1], P('cache'), may hold values from 0 to 31; in each aligned block of 32 rows (0 to 31, 32 to 63, ...) at most 2 rows name the same one
- w_out: bfloat16 [8192, 4096], P('tensor'), may hold values from -1 to 1
Outputs:
- projected: bfloat16 [1024, 32, 4096], P('cache', None, 'tensor')
Inputs may be any that keep to these rules, and one draw needn't show every extreme that they name: `candidate_prefix`: the passage with id p has its cache at prefix_kv[:, p]. Among the candidates of one index of cache at most 2 name the same passage, and exactly 2 do for some passage in some of them.
All inputs are finite; a program needn't handle non-finite values.
Results may differ from a plain program's by a relative error of at most 0.019.
Values may be sent and summed in bfloat16 or wider, within the bound.
No kernel may reach another device: no remote copies, remote signals or barrier semaphores. Data moves between devices by JAX's collectives and lax.ppermute only.
A program may use at most 128 MiB of HBM per device.

v0:
```python
import math

import jax
import jax.numpy as jnp
from jax import lax
from jax.sharding import PartitionSpec as P

H = 64
KVH = 8
HD = 128


def prefix_part(query_rows, key_rows, value_rows):
    row_count = query_rows.shape[0]
    kv_heads = key_rows.shape[1] // HD
    query_heads = query_rows.reshape(row_count, kv_heads, H // KVH, HD)
    key_heads = key_rows.reshape(-1, kv_heads, HD)
    value_heads = value_rows.reshape(-1, kv_heads, HD)
    scores = jnp.einsum(
        "rkgd,lkd->rkgl", query_heads, key_heads, preferred_element_type=jnp.float32
    ) * (1.0 / math.sqrt(HD))
    row_max = jnp.max(scores, axis=-1, keepdims=True)
    exp_scores = jnp.exp(scores - row_max)
    row_total = jnp.sum(exp_scores, axis=-1, keepdims=True)
    weights = exp_scores.astype(jnp.bfloat16)
    summed = jnp.einsum("rkgl,lkd->rkgd", weights, value_heads, preferred_element_type=jnp.float32)
    prefix_out = (summed / row_total).astype(jnp.bfloat16).reshape(row_count, -1)
    return (
        prefix_out,
        row_max[..., 0].reshape(row_count, -1),
        row_total[..., 0].reshape(row_count, -1),
    )


def blocked_prefix(flat_rows, key_rows, value_rows):
    row_count = flat_rows.shape[0]
    block_rows = math.gcd(row_count, 256)
    blocks = flat_rows.reshape(row_count // block_rows, block_rows, flat_rows.shape[1])
    prefix_out, row_max, row_total = lax.map(
        lambda query_rows: prefix_part(query_rows, key_rows, value_rows), blocks
    )
    return (
        prefix_out.reshape(row_count, -1),
        row_max.reshape(row_count, -1),
        row_total.reshape(row_count, -1),
    )


def suffix_part(query_rows, key_rows, value_rows):
    batch, length = (query_rows.shape[0], query_rows.shape[1])
    kv_heads = key_rows.shape[2] // HD
    query_heads = query_rows.reshape(batch, length, kv_heads, H // KVH, HD)
    key_heads = key_rows.reshape(batch, length, kv_heads, HD)
    value_heads = value_rows.reshape(batch, length, kv_heads, HD)
    scores = jnp.einsum(
        "btkgd,bukd->btkgu", query_heads, key_heads, preferred_element_type=jnp.float32
    ) * (1.0 / math.sqrt(HD))
    position = jnp.arange(length)
    causal_mask = (position[:, None] >= position[None, :])[None, :, None, None, :]
    row_max = jnp.max(jnp.where(causal_mask, scores, -jnp.inf), axis=-1, keepdims=True)
    exp_scores = jnp.where(causal_mask, jnp.exp(scores - row_max), 0.0)
    row_total = jnp.sum(exp_scores, axis=-1)
    weights = exp_scores.astype(jnp.bfloat16)
    summed = jnp.einsum(
        "btkgu,bukd->btkgd", weights, value_heads, preferred_element_type=jnp.float32
    )
    return (summed, row_max[..., 0], row_total)


def combine_parts(prefix_out, prefix_max, prefix_total, suffix_sum, suffix_max, suffix_total):
    joint_max = jnp.maximum(prefix_max, suffix_max)
    prefix_gain = prefix_total * jnp.exp(prefix_max - joint_max)
    suffix_gain = jnp.exp(suffix_max - joint_max)
    upper = (
        prefix_gain[..., None] * prefix_out.astype(jnp.float32)
        + suffix_gain[..., None] * suffix_sum
    )
    lower = prefix_gain + suffix_gain * suffix_total
    return (upper / lower[..., None]).astype(jnp.bfloat16)


def shards(queries, prefix_kv, suffix_kv, candidate_prefix, w_out):
    peer_count = lax.axis_size("cache")
    cand_count, suffix_len, query_width = queries.shape
    head_count = query_width // HD
    kv_heads = prefix_kv.shape[3] // HD
    slot_cap = max(2, (2 * cand_count + peer_count - 1) // peer_count)
    prefix_ids = candidate_prefix[:, 0]
    cand_order = jnp.arange(cand_count, dtype=jnp.int32)
    earlier = (prefix_ids[:, None] == prefix_ids[None, :]) & (
        cand_order[None, :] < cand_order[:, None]
    )
    rank_index = jnp.sum(earlier.astype(jnp.int32), axis=1)
    suffix_sum, suffix_max, suffix_total = suffix_part(queries, suffix_kv[0], suffix_kv[1])
    slot_index = prefix_ids * slot_cap + rank_index
    outgoing = jnp.zeros((peer_count * slot_cap, suffix_len, query_width), jnp.bfloat16)
    outgoing = (
        outgoing.at[slot_index].set(queries).reshape(peer_count, slot_cap, suffix_len, query_width)
    )
    key_rows = prefix_kv[0, 0]
    value_rows = prefix_kv[1, 0]
    arrived = lax.all_to_all(outgoing, "cache", split_axis=0, concat_axis=0, tiled=True)
    sources = arrived.shape[0]
    slots = arrived.shape[1]
    flat_rows = arrived.reshape(sources * slots * suffix_len, query_width)
    prefix_out, row_max, row_total = blocked_prefix(flat_rows, key_rows, value_rows)
    back_out = lax.all_to_all(
        prefix_out.reshape(sources, slots, suffix_len, query_width).astype(jnp.float32),
        "cache",
        split_axis=0,
        concat_axis=0,
        tiled=True,
    ).astype(jnp.bfloat16)
    back_max = lax.all_to_all(
        row_max.reshape(sources, slots, suffix_len, head_count),
        "cache",
        split_axis=0,
        concat_axis=0,
        tiled=True,
    )
    back_total = lax.all_to_all(
        row_total.reshape(sources, slots, suffix_len, head_count),
        "cache",
        split_axis=0,
        concat_axis=0,
        tiled=True,
    )
    prefix_out = back_out.reshape(peer_count * slot_cap, suffix_len, query_width)[slot_index]
    prefix_max = back_max.reshape(peer_count * slot_cap, suffix_len, head_count)[slot_index]
    prefix_total = back_total.reshape(peer_count * slot_cap, suffix_len, head_count)[slot_index]
    group = H // KVH
    attention = combine_parts(
        prefix_out.reshape(cand_count, suffix_len, kv_heads, group, HD),
        prefix_max.reshape(cand_count, suffix_len, kv_heads, group),
        prefix_total.reshape(cand_count, suffix_len, kv_heads, group),
        suffix_sum,
        suffix_max,
        suffix_total,
    )
    partial_sum = jnp.dot(
        attention.reshape(cand_count * suffix_len, query_width),
        w_out,
        preferred_element_type=jnp.float32,
    )
    partial_sum = partial_sum.reshape(cand_count, suffix_len, w_out.shape[1])
    return lax.psum_scatter(
        partial_sum.astype(jnp.bfloat16), "tensor", scatter_dimension=2, tiled=True
    )


def solution(mesh):
    in_specs = (
        P("cache", None, "tensor"),
        P(None, "cache", None, "tensor"),
        P(None, "cache", None, "tensor"),
        P("cache", None),
        P("tensor", None),
    )
    out_specs = P("cache", None, "tensor")
    return jax.shard_map(shards, mesh=mesh, in_specs=in_specs, out_specs=out_specs, check_vma=False)
```

profile of v0, /device:TPU:1, one launch (start us, length us, event | category | flops | bytes accessed | tf_op | source)
XLA Modules:
  0.0 383.5 jit_solution(4564776324519183939)
XLA Ops:
  8.2 2.5 broadcast_in_dim.55
  10.7 5.4 %scatter_fusion = bf16[64,32,1024]{2,1,0:T(8,128)(2,1)} fusion(bf16[64,32,1024]{2,1,0:T(8,128)(2,1)} %broadcast_in_dim.55, s32[32]{0:T(128)S(1)} %fusion.43, bf16[32,32,1024]{2,1,0:T(8,128)(2,1)S(1)} %copy-done), kind=kCustom, calls=%fused_computation.3 | custom fusion | bytes 6291584 | tf_op jit(solution)/shard_map/scatter | solution.py:98
  16.1 12.2 %all-to-all-start = ((bf16[32,2,32,1024]{3,2,1,0:T(8,128)(2,1)}), bf16[32,2,32,1024]{3,2,1,0:T(8,128)(2,1)}, u32[]{:S(2)}, u32[]{:S(2)}) async-start(bf16[32,2,32,1024]{3,2,1,0:T(8,128)(2,1)} %bitcast.182), calls=%async_computation | async-start | bytes 8388608 | tf_op jit(solution)/shard_map/all_to_all | solution.py:102
  28.4 92.6 %all-to-all-done = bf16[32,2,32,1024]{3,2,1,0:T(8,128)(2,1)} async-done(((bf16[32,2,32,1024]{3,2,1,0:T(8,128)(2,1)}), bf16[32,2,32,1024]{3,2,1,0:T(8,128)(2,1)}, u32[]{:S(2)}, u32[]{:S(2)}) %all-to-all-start) | async-done | bytes 4194336 | tf_op jit(solution)/shard_map/all_to_all | solution.py:102
  121.0 45.8 %while.14 = (s32[]{:T(128)}, bf16[8,256,1024]{2,1,0:T(8,128)(2,1)}, f32[8,256,8]{1,0,2:T(8,128)S(1)}, f32[8,256,8]{1,0,2:T(8,128)S(1)}, bf16[8,256,1024]{2,1,0:T...) while((s32[]{:T(128)}, bf16[8,256,1024]{2,1,0:T(8,128)(2,1)}, ...), condition=%wide.region_5.6_spmd, body=%wide.region_2.5_spmd.sunk | while | flops 545779712 | bytes 18195048 | solution.py:39
  123.1 1.3 fusion.58
  124.4 1.1 divide_convert_fusion.2
  128.8 1.3 fusion.58
  134.6 1.3 fusion.58
  135.8 1.1 divide_convert_fusion.2
  140.3 1.3 fusion.58
  146.0 1.3 fusion.58
  147.3 1.1 divide_convert_fusion.2
  151.7 1.3 fusion.58
  153.0 1.1 divide_convert_fusion.2
  157.5 1.3 fusion.58
  158.7 1.1 divide_convert_fusion.2
  163.2 1.3 fusion.58
  164.4 1.1 divide_convert_fusion.2
  168.0 9.2 %all-to-all-start.1 = ((f32[32,1,512]{2,1,0:T(1,128)}), f32[32,1,512]{2,1,0:T(1,128)S(1)}, u32[]{:S(2)}, u32[]{:S(2)}) async-start(f32[32,1,512]{2,1,0:T(1,128)} %reshape.217), calls=%async_computation.1 | async-start | bytes 131072 | tf_op jit(solution)/shard_map/all_to_all | solution.py:121
  177.9 8.2 %all-to-all-done.1 = f32[32,1,512]{2,1,0:T(1,128)S(1)} async-done(((f32[32,1,512]{2,1,0:T(1,128)}), f32[32,1,512]{2,1,0:T(1,128)S(1)}, u32[]{:S(2)}, u32[]{:S(2)}) %all-to-all-start.1) | async-done | bytes 65568 | tf_op jit(solution)/shard_map/all_to_all | solution.py:121
  186.1 12.1 %all_to_all.20 = f32[32,1,512]{2,1,0:T(1,128)S(1)} all-to-all(f32[32,1,512]{2,1,0:T(1,128)S(1)} %reshape.219), channel_id=1, replica_groups=mesh['cache'=32,'tensor'=8] {'cache'}, dimensions={0} | all-to-all | bytes 131072 | tf_op jit(solution)/shard_map/all_to_all | solution.py:114
  198.2 5.0 %all-to-all-start.3 = ((bf16[32,2,32,1024]{3,2,1,0:T(8,128)(2,1)}), bf16[32,2,32,1024]{3,2,1,0:T(8,128)(2,1)}, u32[]{:S(2)}, u32[]{:S(2)}) async-start(bf16[32,2,32,1024]{3,2,1,0:T(8,128)(2,1)} %bitcast.186), calls=%async_computation.3 | async-start | bytes 8388608 | tf_op jit(solution)/shard_map/all_to_all | solution.py:107
  203.4 3.3 fusion.26
  206.7 1.7 fusion.29
  208.4 3.1 copy.65
  216.9 78.0 %all-to-all-done.3 = bf16[32,2,32,1024]{3,2,1,0:T(8,128)(2,1)} async-done(((bf16[32,2,32,1024]{3,2,1,0:T(8,128)(2,1)}), bf16[32,2,32,1024]{3,2,1,0:T(8,128)(2,1)}, u32[]{:S(2)}, u32[]{:S(2)}) %all-to-all-start.3) | async-done | bytes 4194336 | tf_op jit(solution)/shard_map/all_to_all | solution.py:107
  294.9 2.9 gather_fusion.2
  299.6 4.0 %fusion.25 = bf16[32,32,1,8,128]{4,3,1,0,2:T(8,128)(2,1)S(1)} fusion(f32[32,32,1,8,128]{4,3,1,0,2:T(8,128)S(1)} %bitcast.185, bf16[32,32,8,32]{3,2,1,0:T(8,128)(2,1)S(1)} %copy-done.1, f32[32,32,8]{2,1,0:T(8,128)S(1)} %copy-done.2, f32[32,32,8]{2,1,0:T(8,128)S(1)} %copy.64, f32[32,32,8]{2,1,0:T(8,128)S(1)} %copy.62, bf16[2,32,32,128]{3,2,1,0:T(8,128)(2,1)S(1)} %copy-done.5), kind=kOutput, calls=%fused_computation.28 | convolution fusion | flops 72351744 | bytes 10223616 | tf_op jit(solution)/shard_map/btkgu,bukd->btkgd/dot_general | solution.py:64
  303.6 2.4 dot_general.29
  306.0 14.7 %fusion.19 = bf16[32,32,4096]{2,1,0:T(8,128)(2,1)} fusion(bf16[32,32,1024]{2,1,0:T(8,128)(2,1)} %dot_general.29, bf16[1024,4096]{1,0:T(8,128)(2,1)} %param.11), kind=kOutput, calls=%fused_computation.23 | convolution fusion | flops 8594128896 | bytes 18874368 | tf_op jit(solution)/shard_map/dot_general | solution.py:140
  320.7 56.0 %reduce-scatter.2.cloned.1.call-done = bf16[32,32,512]{2,1,0:T(8,128)(2,1)} async-done(((bf16[32,32,4096]{2,1,0:T(8,128)(2,1)}), bf16[32,32,512]{2,1,0:T(8,128)(2,1)}) %reduce-scatter.2.cloned.1.call-update) | async-done | bytes 1048592 | tf_op jit(solution)/shard_map/reduce_scatter | solution.py:146
  (121 shorter events, 39.5 us)
Async XLA Ops:
  6.5 4.2 %copy-start = (bf16[32,32,1024]{2,1,0:T(8,128)(2,1)S(1)}, bf16[32,32,1024]{2,1,0:T(8,128)(2,1)}, u32[]{:S(2)}) copy-start(bf16[32,32,1024]{2,1,0:T(8,128)(2,1)} %param.7) | copy-start | bytes 6291460
  8.2 7.9 %copy-start.6 = (s32[32]{0:T(128)}, s32[32]{0:T(128)S(1)}, u32[]{:S(2)}) copy-start(s32[32]{0:T(128)S(1)} %fusion.43) | copy-start | bytes 388
  16.1 12.2 %copy-start.3 = (bf16[2,1,512,128]{3,2,1,0:T(8,128)(2,1)S(1)}, bf16[2,1,512,128]{3,2,1,0:T(8,128)(2,1)}, u32[]{:S(2)}) copy-start(bf16[2,1,512,128]{3,2,1,0:T(8,128)(2,1)} %param.8) | copy-start | bytes 786436
  16.1 104.9 %all-to-all-start = ((bf16[32,2,32,1024]{3,2,1,0:T(8,128)(2,1)}), bf16[32,2,32,1024]{3,2,1,0:T(8,128)(2,1)}, u32[]{:S(2)}, u32[]{:S(2)}) async-start(bf16[32,2,32,1024]{3,2,1,0:T(8,128)(2,1)} %bitcast.182), calls=%async_computation | async-start | bytes 8388608 | tf_op jit(solution)/shard_map/all_to_all | solution.py:102
  168.0 18.1 %all-to-all-start.1 = ((f32[32,1,512]{2,1,0:T(1,128)}), f32[32,1,512]{2,1,0:T(1,128)S(1)}, u32[]{:S(2)}, u32[]{:S(2)}) async-start(f32[32,1,512]{2,1,0:T(1,128)} %reshape.217), calls=%async_computation.1 | async-start | bytes 131072 | tf_op jit(solution)/shard_map/all_to_all | solution.py:121
  198.2 5.2 %copy-start.4 = (bf16[2,32,32,128]{3,2,1,0:T(8,128)(2,1)S(1)}, bf16[2,32,32,128]{3,2,1,0:T(8,128)(2,1)}, u32[]{:S(2)}) copy-start(bf16[2,32,32,128]{3,2,1,0:T(8,128)(2,1)} %param.9) | copy-start | bytes 1572868
  198.2 96.7 %all-to-all-start.3 = ((bf16[32,2,32,1024]{3,2,1,0:T(8,128)(2,1)}), bf16[32,2,32,1024]{3,2,1,0:T(8,128)(2,1)}, u32[]{:S(2)}, u32[]{:S(2)}) async-start(bf16[32,2,32,1024]{3,2,1,0:T(8,128)(2,1)} %bitcast.186), calls=%async_computation.3 | async-start | bytes 8388608 | tf_op jit(solution)/shard_map/all_to_all | solution.py:107
  203.2 173.5 %reduce-scatter.2.cloned.1.call-start = ((), (), s32[]{:S(2)}) async-start(), calls=%async_computation.5 | async-start | bytes 9437184 | tf_op jit(solution)/shard_map/reduce_scatter | solution.py:146
  206.7 4.8 %copy-start.7 = (s32[32]{0:T(128)S(1)}, s32[32]{0:T(128)}, u32[]{:S(2)}) copy-start(s32[32]{0:T(128)} %copy-done.6) | copy-start | bytes 388
  297.8 1.6 copy-start.1
  297.8 1.7 copy-start.2
  297.8 1.8 copy-start.5
Sparse Core Ops, SparseCore 0:
  320.8 55.8 reduce-scatter.1
where the time goes:
time: 384 us
  waiting for transfers between devices  235 us (61%)
  local copies, waits for them, and re-layouts  43.4 us (11%)
  matrix products  37.3 us (10%)
  starting transfers between devices  26.6 us (7%)
  other arithmetic  15.1 us (4%)
  between operations  13.7 us (4%)
  blocking collectives  12.1 us (3%)
    all_to_all x1, waiting for transfers between devices, shards(): lax.all_to_all(outgoing, 'cache', split_axis=0, concat_axis=0, tiled=True)  92.6 us
    all_to_all x1, waiting for transfers between devices, shards(): lax.all_to_all(prefix_out.reshape(sources, slots, suffix_len, query_width...  78 us
    reduce_scatter x1, waiting for transfers between devices, shards(): lax.psum_scatter(partial_sum.astype(jnp.bfloat16), 'tensor', scatter_dime...  56 us
    dot_general x1, matrix products, shards(): jnp.dot(attention.reshape(cand_count * suffix_len, query_width), w_out, p...  14.7 us
    all_to_all x1, starting transfers between devices, shards(): lax.all_to_all(outgoing, 'cache', split_axis=0, concat_axis=0, tiled=True)  12.2 us
    all_to_all x1, blocking collectives, shards(): lax.all_to_all(row_max.reshape(sources, slots, suffix_len, head_count), '...  12.1 us
    dynamic_slice x16, local copies, waits for them, and re-layouts, blocked_prefix(): lax.map(lambda query_rows: prefix_part(query_rows, key_rows, value_rows),...  10.3 us
    reduce_sum x8, other arithmetic, prefix_part(): row_total = jnp.sum(exp_scores, axis=-1, keepdims=True)  10.1 us
  transfers between devices with their start and end apart: 4, of which 4 were waited for; matrix products, arithmetic and copies ran while one was open for 4% of the time, Pallas kernels for 0%

commit v1 on v0

v1 whole, which is shorter than its diff:
```python
import functools
import math

import jax
import jax.numpy as jnp
from jax import lax
from jax.experimental import pallas as pl
from jax.experimental.pallas import tpu as pltpu
from jax.sharding import PartitionSpec as P

H = 64
KVH = 8
HD = 128
GROUP = H // KVH
NX = 4
NZ = 8
NY = 4
LOG2E = 1.4426950408889634
MIB = 1024 * 1024


def send_cache(value, step_x, step_z):
    pairs = [
        (x * NZ + z, ((x + step_x) % NX) * NZ + (z + step_z) % NZ)
        for x in range(NX)
        for z in range(NZ)
    ]
    return lax.ppermute(value, "cache", pairs)


def send_y(value, step):
    pairs = [(2 * y + c, 2 * ((y + step) % NY) + c) for y in range(NY) for c in range(2)]
    return lax.ppermute(value, "tensor", pairs)


def swap_core(value):
    return lax.ppermute(value, "tensor", [(t, t ^ 1) for t in range(2 * NY)])


def gather_prefix(block):
    pieces = []

    def whole(array, dz, dx):
        for kv in range(2):
            pieces.append((array, kv, kv, (dz % NZ) * NX + dx % NX, 0))

    def part(array, at, kv, dz, dx, first=0):
        pieces.append((array, at, kv, (dz % NZ) * NX + dx % NX, first))

    whole(block, 0, 0)
    from_z = {}
    from_x = {}
    from_z[1] = send_cache(block, 0, -1)
    from_z[-1] = send_cache(block, 0, 1)
    from_x[1] = send_cache(block, -1, 0)
    from_x[-1] = send_cache(block, 1, 0)
    whole(from_x[1], 0, 1)
    whole(from_x[-1], 0, -1)
    key_x2 = send_cache(from_x[1][0:1], -1, 0)
    value_x2 = send_cache(from_x[-1][1:2], 1, 0)
    part(key_x2, 0, 0, 0, 2)
    part(value_x2, 0, 1, 0, 2)
    for step in (2, 3):
        from_z[step] = send_cache(from_z[step - 1], 0, -1)
        from_z[-step] = send_cache(from_z[1 - step], 0, 1)
    for step in (1, 2, 3):
        whole(from_z[step], step, 0)
        whole(from_z[-step], -step, 0)
    key_z4 = send_cache(from_z[3][0:1], 0, -1)
    value_z4 = send_cache(from_z[-3][1:2], 0, 1)
    part(key_z4, 0, 0, 4, 0)
    part(value_z4, 0, 1, 4, 0)

    values = jnp.concatenate([from_x[1][1:2], from_x[-1][1:2], value_x2], axis=0)
    dxs = (1, -1, 2)
    ahead, behind = values, values
    for step in (1, 2, 3):
        ahead = send_cache(ahead, 0, -1)
        behind = send_cache(behind, 0, 1)
        for at, dx in enumerate(dxs):
            part(ahead, at, 1, step, dx)
            part(behind, at, 1, -step, dx)
    length = block.shape[1]
    half = length // 2
    upper = send_cache(ahead[:, :half], 0, -1)
    lower = send_cache(behind[:, half:], 0, 1)
    for at, dx in enumerate(dxs):
        part(upper, at, 1, 4, dx, 0)
        part(lower, at, 1, 4, dx, half)

    near = jnp.concatenate(
        [from_z[1][0:1], from_z[-1][0:1], from_z[2][0:1], from_z[-2][0:1]], axis=0
    )
    ahead, behind = send_cache(near, -1, 0), send_cache(near, 1, 0)
    far_a, far_b = send_cache(ahead[:2], -1, 0), send_cache(behind[2:], 1, 0)
    for at, dz in enumerate((1, -1, 2, -2)):
        part(ahead, at, 0, dz, 1)
        part(behind, at, 0, dz, -1)
        part(far_a if at < 2 else far_b, at % 2, 0, dz, 2)
    distant = jnp.concatenate([from_z[3][0:1], from_z[-3][0:1], key_z4], axis=0)
    ahead, behind = send_cache(distant, -1, 0), send_cache(distant, 1, 0)
    upper, lower = send_cache(ahead[:, :half], -1, 0), send_cache(behind[:, half:], 1, 0)
    for at, dz in enumerate((3, -3, 4)):
        part(ahead, at, 0, dz, 1)
        part(behind, at, 0, dz, -1)
        part(upper, at, 0, dz, 2, 0)
        part(lower, at, 0, dz, 2, half)
    return pieces


def attention_kernel(places, n_arrays, per_step, codes, q_ref, s_ref, *rest):
    arrays = rest[:n_arrays]
    o_ref, cache, sems = rest[n_arrays:]
    step = pl.program_id(0)

    def copies():
        for n, (which, at, kv, code, first) in enumerate(places):
            rows = arrays[which].shape[1]
            yield pltpu.make_async_copy(
                arrays[which].at[at],
                cache.at[kv, code, pl.ds(first, rows)],
                sems.at[n],
            )

    @pl.when(step == 0)
    def _():
        for copy in copies():
            copy.start()
        for copy in copies():
            copy.wait()

    suffix = q_ref.shape[1]
    rows = GROUP * suffix
    factor = LOG2E / math.sqrt(HD)
    token = lax.broadcasted_iota(jnp.int32, (rows, suffix), 0) % suffix
    other = lax.broadcasted_iota(jnp.int32, (rows, suffix), 1)
    causal = other <= token
    contract_last = (((1,), (1,)), ((), ()))
    contract = (((1,), (0,)), ((), ()))
    for i in range(per_step):
        code = codes[step * per_step + i]
        q = jnp.concatenate([q_ref[i, :, g * HD : (g + 1) * HD] for g in range(GROUP)], axis=0)
        far = lax.dot_general(q, cache[0, code], contract_last, preferred_element_type=jnp.float32)
        near = lax.dot_general(q, s_ref[0, i], contract_last, preferred_element_type=jnp.float32)
        near = jnp.where(causal, near, -jnp.inf)
        top = jnp.maximum(
            jnp.max(far, axis=1, keepdims=True), jnp.max(near, axis=1, keepdims=True)
        )
        far = jnp.exp2((far - top) * factor)
        near = jnp.exp2((near - top) * factor)
        total = jnp.sum(far, axis=1, keepdims=True) + jnp.sum(near, axis=1, keepdims=True)
        summed = lax.dot_general(
            far.astype(jnp.bfloat16), cache[1, code], contract, preferred_element_type=jnp.float32
        ) + lax.dot_general(
            near.astype(jnp.bfloat16), s_ref[1, i], contract, preferred_element_type=jnp.float32
        )
        out = (summed / total).astype(jnp.bfloat16)
        for g in range(GROUP):
            o_ref[i, :, g * HD : (g + 1) * HD] = out[g * suffix : (g + 1) * suffix]


def attend(codes, queries, suffix_kv, pieces, length):
    arrays = []
    places = []
    for array, at, kv, code, first in pieces:
        which = next((n for n, a in enumerate(arrays) if a is array), len(arrays))
        if which == len(arrays):
            arrays.append(array)
        places.append((which, at, kv, code, first))
    count, suffix, width = queries.shape
    per_step = 2
    return pl.pallas_call(
        functools.partial(attention_kernel, places, len(arrays), per_step),
        out_shape=jax.ShapeDtypeStruct(queries.shape, jnp.bfloat16),
        grid_spec=pltpu.PrefetchScalarGridSpec(
            num_scalar_prefetch=1,
            grid=(count // per_step,),
            in_specs=[
                pl.BlockSpec((per_step, suffix, width), lambda n, c: (n, 0, 0)),
                pl.BlockSpec((2, per_step, suffix, HD), lambda n, c: (0, n, 0, 0)),
            ]
            + [pl.BlockSpec(memory_space=pl.ANY)] * len(arrays),
            out_specs=pl.BlockSpec((per_step, suffix, width), lambda n, c: (n, 0, 0)),
            scratch_shapes=[
                pltpu.VMEM((2, NX * NZ, length, HD), jnp.bfloat16),
                pltpu.SemaphoreType.DMA((len(places),)),
            ],
        ),
        compiler_params=pltpu.CompilerParams(vmem_limit_bytes=24 * MIB),
        cost_estimate=pl.CostEstimate(
            flops=4 * count * suffix * width * length,
            bytes_accessed=16 * MIB,
            transcendentals=count * suffix * GROUP * length,
        ),
    )(codes, queries, suffix_kv, *arrays)


def pick_kernel(place, w_ref, o_ref):
    o_ref[0] = w_ref[...]


def pick_columns(place, w_out, width):
    depth = w_out.shape[0]
    return pl.pallas_call(
        pick_kernel,
        out_shape=jax.ShapeDtypeStruct((NY, depth, width), w_out.dtype),
        grid_spec=pltpu.PrefetchScalarGridSpec(
            num_scalar_prefetch=1,
            grid=(NY,),
            in_specs=[pl.BlockSpec((depth, width), lambda n, p: (0, 2 * n + 1 - p[1]))],
            out_specs=pl.BlockSpec((1, depth, width), lambda n, p: (n, 0, 0)),
        ),
        compiler_params=pltpu.CompilerParams(vmem_limit_bytes=8 * MIB),
        cost_estimate=pl.CostEstimate(flops=0, bytes_accessed=8 * MIB, transcendentals=0),
    )(place, w_out)


def project_kernel(place, a_ref, b_ref, wa_ref, wb_ref, o_ref):
    total = jnp.dot(a_ref[...], wa_ref[...], preferred_element_type=jnp.float32)
    total += jnp.dot(b_ref[...], wb_ref[0], preferred_element_type=jnp.float32)
    o_ref[...] = total.astype(jnp.bfloat16)


def project(place, mine, mate, w_out, w_mate, turn, first, rows):
    depth, width = w_mate.shape[1:]
    tile = min(256, rows)
    base = first // tile

    def column(n, p):
        return (0, 2 * ((p[0] + turn) % NY) + p[1])

    def block(n, p):
        return ((p[0] + turn) % NY, 0, 0)

    return pl.pallas_call(
        project_kernel,
        out_shape=jax.ShapeDtypeStruct((rows, width), jnp.bfloat16),
        grid_spec=pltpu.PrefetchScalarGridSpec(
            num_scalar_prefetch=1,
            grid=(rows // tile,),
            in_specs=[
                pl.BlockSpec((tile, depth), lambda n, p: (base + n, 0)),
                pl.BlockSpec((tile, depth), lambda n, p: (base + n, 0)),
                pl.BlockSpec((depth, width), column),
                pl.BlockSpec((1, depth, width), block),
            ],
            out_specs=pl.BlockSpec((tile, width), lambda n, p: (n, 0)),
        ),
        compiler_params=pltpu.CompilerParams(vmem_limit_bytes=16 * MIB),
        cost_estimate=pl.CostEstimate(
            flops=4 * rows * depth * width, bytes_accessed=6 * MIB, transcendentals=0
        ),
    )(place, mine, mate, w_out, w_mate)


def added(*terms):
    return sum(t.astype(jnp.float32) for t in terms).astype(jnp.bfloat16)


def shards(queries, prefix_kv, suffix_kv, candidate_prefix, w_out):
    count, suffix, width = queries.shape
    length = prefix_kv.shape[2]
    out_width = w_out.shape[1] // (2 * NY)
    me = lax.axis_index("cache")
    t = lax.axis_index("tensor")
    place = jnp.stack([t // 2, t % 2]).astype(jnp.int32)
    ids = candidate_prefix[:, 0]
    codes = ((ids % NZ - me % NZ) % NZ) * NX + (ids // NZ - me // NZ) % NX

    pieces = gather_prefix(prefix_kv.reshape(2, length, HD))
    w_mate = swap_core(pick_columns(place, w_out, out_width))
    mine = attend(codes, queries, suffix_kv, pieces, length).reshape(count * suffix, width)
    mate = swap_core(mine)

    rows = count * suffix
    half = rows // 2
    part = functools.partial(project, place, mine, mate, w_out, w_mate)
    top2 = send_y(part(2, 0, half), 1)
    low2 = send_y(part(2, half, half), -1)
    low1 = send_y(part(1, half, half), 1)
    top3 = send_y(part(3, 0, half), -1)
    own_top1 = part(1, 0, half)
    own_low3 = part(3, half, half)
    top1 = send_y(added(own_top1, top2), 1)
    low3 = send_y(added(own_low3, low2), -1)
    own_top = part(0, 0, half)
    own_low = part(0, half, half)
    top = added(own_top, top1, top3)
    low = added(own_low, low1, low3)
    return jnp.concatenate([top, low], axis=0).reshape(count, suffix, out_width)


def solution(mesh):
    in_specs = (
        P("cache", None, "tensor"),
        P(None, "cache", None, "tensor"),
        P(None, "cache", None, "tensor"),
        P("cache", None),
        P("tensor", None),
    )
    out_specs = P("cache", None, "tensor")
    return jax.shard_map(shards, mesh=mesh, in_specs=in_specs, out_specs=out_specs, check_vma=False)
```

time: 384 us -> 183 us (0.48)
  waiting for transfers between devices: 235 us -> 43.9 us
  Pallas kernels: 0 us -> 56.6 us
  matrix products: 37.3 us -> 0 us
  starting transfers between devices: 26.6 us -> 50 us
  local copies, waits for them, and re-layouts: 43.4 us -> 27.7 us
  between operations: 13.7 us -> 0.38 us
  other arithmetic: 15.1 us -> 1.99 us
  blocking collectives: 12.1 us -> 0 us
    all_to_all x3 -> x0, waiting for transfers between devices: 179 us -> none  [the longest x1 92.6 us: shards(): lax.all_to_all(outgoing, 'cache', split_axis=0, concat_axis=0, tiled=True)]
    pallas_call x0 -> x10, Pallas kernels: none -> 56.6 us  [the longest x8 26.7 us: project(): pl.pallas_call(project_kernel, out_shape=jax.ShapeDtypeStruct((rows, widt...]
    reduce_scatter x1 -> x0, waiting for transfers between devices: 56 us -> none  [shards(): lax.psum_scatter(partial_sum.astype(jnp.bfloat16), 'tensor', scatter_dime...]
    ppermute x0 -> x36, starting transfers between devices: none -> 50 us  [the longest x28 35.4 us: send_cache(): return lax.ppermute(value, 'cache', pairs)]
    ppermute x0 -> x36, waiting for transfers between devices: none -> 43.9 us  [the longest x28 29.9 us: send_cache(): return lax.ppermute(value, 'cache', pairs)]
    dot_general x19 -> x0, matrix products: 37.3 us -> none  [the longest x1 14.7 us: shards(): jnp.dot(attention.reshape(cand_count * suffix_len, query_width), w_out, p...]
    all_to_all x3 -> x0, starting transfers between devices: 26.4 us -> none  [the longest x1 12.2 us: shards(): lax.all_to_all(outgoing, 'cache', split_axis=0, concat_axis=0, tiled=True)]
    unnamed x22 -> x60, local copies, waits for them, and re-layouts: 3.57 us -> 21.1 us
  transfers between devices with their start and end apart: 4 -> 36, of which waited for: 4 -> 15; matrix products, arithmetic and copies ran while one was open for 4% -> 4% of each run, Pallas kernels for 0% -> 29%
where the time goes in v1:
time: 183 us; the launch traced here: 181 us
  Pallas kernels  56.6 us (31%)
  starting transfers between devices  50 us (27%)
  waiting for transfers between devices  43.9 us (24%)
  local copies, waits for them, and re-layouts  27.7 us (15%)
  other arithmetic  1.99 us (1%)
    ppermute x28, starting transfers between devices, send_cache(): return lax.ppermute(value, 'cache', pairs)  35.4 us
    ppermute x28, waiting for transfers between devices, send_cache(): return lax.ppermute(value, 'cache', pairs)  29.9 us
    pallas_call x8, Pallas kernels, project(): pl.pallas_call(project_kernel, out_shape=jax.ShapeDtypeStruct((rows, widt...  26.7 us
    pallas_call x1, Pallas kernels, attend(): pl.pallas_call(functools.partial(attention_kernel, places, len(arrays), p...  26.6 us
    unnamed x60, local copies, waits for them, and re-layouts  21.1 us
    ppermute x6, waiting for transfers between devices, send_y(): return lax.ppermute(value, 'tensor', pairs)  10.2 us
    ppermute x6, starting transfers between devices, send_y(): return lax.ppermute(value, 'tensor', pairs)  7.45 us
    ppermute x2, starting transfers between devices, swap_core(): return lax.ppermute(value, 'tensor', [(t, t ^ 1) for t in range(2 * NY)])  7.18 us
  transfers between devices with their start and end apart: 36, of which 15 were waited for; matrix products, arithmetic and copies ran while one was open for 4% of the time, Pallas kernels for 29%

profile of v1, /device:TPU:1, one launch (start us, length us, event | category | flops | bytes accessed | tf_op | source)
XLA Modules:
  0.0 180.6 jit_solution(1414184354400547350)
XLA Ops:
  0.0 2.0 %collective-permute-start.1 = (bf16[2,512,128]{2,1,0:T(8,128)(2,1)}, bf16[2,512,128]{2,1,0:T(8,128)(2,1)S(1)}, u32[]{:S(2)}, u32[]{:S(2)}) collective-permute-start(bf16[2,512,128]{2,1,0:T(8,128)(2,1)} %bitcast.27), channel_id=1, source_target_pairs={{0,64},{8,72},{16,80},{24,88},{32,96},{40,104},{48,112},{56,120},{... | collective-permute-start | bytes 786440 | tf_op jit(solution)/shard_map/ppermute | solution.py:28
  3.7 3.9 %collective-permute-start.4 = (bf16[2,512,128]{2,1,0:T(8,128)(2,1)}, bf16[2,512,128]{2,1,0:T(8,128)(2,1)S(1)}, u32[]{:S(2)}, u32[]{:S(2)}) collective-permute-start(bf16[2,512,128]{2,1,0:T(8,128)(2,1)} %bitcast.29), channel_id=1, source_target_pairs={{0,56},{8,0},{16,8},{24,16},{32,24},{40,32},{48,40},{56,48},{64,12... | collective-permute-start | bytes 786440 | tf_op jit(solution)/shard_map/ppermute | solution.py:28
  9.2 3.4 %copy-done = bf16[1024,4096]{1,0:T(8,128)(2,1)S(1)} copy-done((bf16[1024,4096]{1,0:T(8,128)(2,1)S(1)}, bf16[1024,4096]{1,0:T(8,128)(2,1)}, u32[]{:S(2)}) %copy-start) | copy-done | bytes 8388632
  12.5 3.3 %shard_map.56 = bf16[4,1024,512]{2,1,0:T(8,128)(2,1)} custom-call(s32[2]{0:T(128)S(1)} %pad_add_fusion.place, bf16[1024,4096]{1,0:T(8,128)(2,1)S(1)} %copy-done), custom_call_target="tpu_custom_call" | custom-call | bytes 8388608 | tf_op jit(solution)/shard_map/pallas_call | solution.py:204
  17.6 2.6 %collective-permute-start.6 = (bf16[2,512,128]{2,1,0:T(8,128)(2,1)S(1)}, bf16[2,512,128]{2,1,0:T(8,128)(2,1)S(1)}, u32[]{:S(2)}, u32[]{:S(2)}) collective-permute-start(bf16[2,512,128]{2,1,0:T(8,128)(2,1)S(1)} %collective-permute-done.4.rest_5_), channel_id=1, source_target_pairs={{0,56},{8,0},{16,8},{24,16},{32,24},{40,32},{48,40},{56,48},{64,12... | collective-permute-start | bytes 786440 | tf_op jit(solution)/shard_map/ppermute | solution.py:28
  20.9 2.9 %collective-permute-done.3.rest_4_ = bf16[1,512,128]{2,1,0:T(8,128)(2,1)S(1)} collective-permute-done((bf16[1,512,128]{2,1,0:T(8,128)(2,1)S(1)}, bf16[1,512,128]{2,1,0:T(8,128)(2,1)S(1)}, u32[]{:S(2)}, u32[]{:S(2)}) %collective-permute-start.3) | collective-permute-done | bytes 131104 | tf_op jit(solution)/shard_map/ppermute | solution.py:28
  24.0 2.6 %collective-permute-done.7.rest_8_ = bf16[2,512,128]{2,1,0:T(8,128)(2,1)S(1)} collective-permute-done((bf16[2,512,128]{2,1,0:T(8,128)(2,1)S(1)}, bf16[2,512,128]{2,1,0:T(8,128)(2,1)S(1)}, u32[]{:S(2)}, u32[]{:S(2)}) %collective-permute-start.7) | collective-permute-done | bytes 262176 | tf_op jit(solution)/shard_map/ppermute | solution.py:28
  26.6 2.7 %collective-permute-start.8 = (bf16[2,512,128]{2,1,0:T(8,128)(2,1)S(1)}, bf16[2,512,128]{2,1,0:T(8,128)(2,1)S(1)}, u32[]{:S(2)}, u32[]{:S(2)}) collective-permute-start(bf16[2,512,128]{2,1,0:T(8,128)(2,1)S(1)} %collective-permute-done.6.rest_7_), channel_id=1, source_target_pairs={{0,56},{8,0},{16,8},{24,16},{32,24},{40,32},{48,40},{56,48},{64,12... | collective-permute-start | bytes 786440 | tf_op jit(solution)/shard_map/ppermute | solution.py:28
  29.5 11.1 %collective-permute-done.9.rest_10_ = bf16[2,512,128]{2,1,0:T(8,128)(2,1)S(1)} collective-permute-done((bf16[2,512,128]{2,1,0:T(8,128)(2,1)S(1)}, bf16[2,512,128]{2,1,0:T(8,128)(2,1)S(1)}, u32[]{:S(2)}, u32[]{:S(2)}) %collective-permute-start.9) | collective-permute-done | bytes 262176 | tf_op jit(solution)/shard_map/ppermute | solution.py:28
  45.0 2.6 %collective-permute-done.10.rest_11_ = bf16[1,512,128]{2,1,0:T(8,128)(2,1)S(1)} collective-permute-done((bf16[1,512,128]{2,1,0:T(8,128)(2,1)S(1)}, bf16[1,512,128]{2,1,0:T(8,128)(2,1)S(1)}, u32[]{:S(2)}, u32[]{:S(2)}) %collective-permute-start.10) | collective-permute-done | bytes 131104 | tf_op jit(solution)/shard_map/ppermute | solution.py:28
  50.1 3.5 %collective-permute-done.21.rest_22_ = bf16[4,512,128]{2,1,0:T(8,128)(2,1)S(1)} collective-permute-done((bf16[4,512,128]{2,1,0:T(8,128)(2,1)S(1)}, bf16[4,512,128]{2,1,0:T(8,128)(2,1)S(1)}, u32[]{:S(2)}, u32[]{:S(2)}) %collective-permute-start.21) | collective-permute-done | bytes 524320 | tf_op jit(solution)/shard_map/ppermute | solution.py:28
  53.9 2.4 %collective-permute-start.24 = (bf16[3,512,128]{2,1,0:T(8,128)(2,1)S(1)}, bf16[3,512,128]{2,1,0:T(8,128)(2,1)}, u32[]{:S(2)}, u32[]{:S(2)}) collective-permute-start(bf16[3,512,128]{2,1,0:T(8,128)(2,1)S(1)} %pad_maximum_fusion.3), channel_id=1, source_target_pairs={{0,192},{8,200},{16,208},{24,216},{32,224},{40,232},{48,240},{56,2... | collective-permute-start | bytes 1179656 | tf_op jit(solution)/shard_map/ppermute | solution.py:28
  57.1 2.7 %collective-permute-start.16 = (bf16[3,512,128]{2,1,0:T(8,128)(2,1)S(1)}, bf16[3,512,128]{2,1,0:T(8,128)(2,1)}, u32[]{:S(2)}, u32[]{:S(2)}) collective-permute-start(bf16[3,512,128]{2,1,0:T(8,128)(2,1)S(1)} %collective-permute-done.14.rest_15_), channel_id=1, source_target_pairs={{0,56},{8,0},{16,8},{24,16},{32,24},{40,32},{48,40},{56,48},{64,12... | collective-permute-start | bytes 1179656 | tf_op jit(solution)/shard_map/ppermute | solution.py:28
  62.9 2.7 %collective-permute-start.22 = (bf16[2,512,128]{2,1,0:T(8,128)(2,1)}, bf16[2,512,128]{2,1,0:T(8,128)(2,1)}, u32[]{:S(2)}, u32[]{:S(2)}) collective-permute-start(bf16[2,512,128]{2,1,0:T(8,128)(2,1)} %slice.77), channel_id=1, source_target_pairs={{0,192},{8,200},{16,208},{24,216},{32,224},{40,232},{48,240},{56,2... | collective-permute-start | bytes 786440 | tf_op jit(solution)/shard_map/ppermute | solution.py:28
  73.7 1.9 %collective-permute-start.19 = (bf16[3,256,128]{2,1,0:T(8,128)(2,1)S(1)}, bf16[3,256,128]{2,1,0:T(8,128)(2,1)S(1)}, u32[]{:S(2)}, u32[]{:S(2)}) collective-permute-start(bf16[3,256,128]{2,1,0:T(8,128)(2,1)S(1)} %slice.72), channel_id=1, source_target_pairs={{0,8},{8,16},{16,24},{24,32},{32,40},{40,48},{48,56},{56,0},{64,72... | collective-permute-start | bytes 589832 | tf_op jit(solution)/shard_map/ppermute | solution.py:28
  76.9 2.6 %collective-permute-done.19.rest_20_ = bf16[3,256,128]{2,1,0:T(8,128)(2,1)S(1)} collective-permute-done((bf16[3,256,128]{2,1,0:T(8,128)(2,1)S(1)}, bf16[3,256,128]{2,1,0:T(8,128)(2,1)S(1)}, u32[]{:S(2)}, u32[]{:S(2)}) %collective-permute-start.19) | collective-permute-done | bytes 196640 | tf_op jit(solution)/shard_map/ppermute | solution.py:28
  79.5 1.9 %collective-permute-done.18.rest_19_ = bf16[3,256,128]{2,1,0:T(8,128)(2,1)S(1)} collective-permute-done((bf16[3,256,128]{2,1,0:T(8,128)(2,1)S(1)}, bf16[3,256,128]{2,1,0:T(8,128)(2,1)S(1)}, u32[]{:S(2)}, u32[]{:S(2)}) %collective-permute-start.18) | collective-permute-done | bytes 196640 | tf_op jit(solution)/shard_map/ppermute | solution.py:28
  95.0 26.6 %shard_map.55 = bf16[32,32,1024]{2,1,0:T(8,128)(2,1)S(1)} custom-call(s32[32]{0:T(128)S(1)} %fusion.codes, bf16[32,32,1024]{2,1,0:T(8,128)(2,1)S(1)} %copy-done.2, bf16[2,32,32,128]{3,2,1,0:T(8,128)(2,1)S(1)} %copy-done.19, bf16[2,512,128]{2,1,0:T(8,128)(2,1)S(1)} %bitcast.31, bf16[2,512,128]{2,1,0:T(8,128)(2,1)S(1)} %collective-permute-done.rest_1_, ...), custom_call_target="tpu_custom_call" | custom-call | flops 2147483648 | bytes 16777216 | tf_op jit(solution)/shard_map/pallas_call | solution.py:172
  121.6 5.7 %collective-permute-start.28 = (bf16[1024,1024]{1,0:T(8,128)(2,1)S(1)}, bf16[1024,1024]{1,0:T(8,128)(2,1)S(1)}, u32[]{:S(2)}, u32[]{:S(2)}) collective-permute-start(bf16[1024,1024]{1,0:T(8,128)(2,1)S(1)} %bitcast.18), channel_id=1, source_target_pairs={{0,1},{1,0},{2,3},{3,2},{4,5},{5,4},{6,7},{7,6},{8,9},{9,8},{10,11... | collective-permute-start | bytes 6291464 | tf_op jit(solution)/shard_map/ppermute | solution.py:37
  127.2 3.8 %collective-permute-done.28.b_ref = bf16[1024,1024]{1,0:T(8,128)(2,1)S(1)} collective-permute-done((bf16[1024,1024]{1,0:T(8,128)(2,1)S(1)}, bf16[1024,1024]{1,0:T(8,128)(2,1)S(1)}, u32[]{:S(2)}, u32[]{:S(2)}) %collective-permute-start.28) | collective-permute-done | bytes 2097184 | tf_op jit(solution)/shard_map/ppermute | solution.py:37
  131.0 3.4 %copy-done.1 = bf16[1024,4096]{1,0:T(8,128)(2,1)S(1)} copy-done((bf16[1024,4096]{1,0:T(8,128)(2,1)S(1)}, bf16[1024,4096]{1,0:T(8,128)(2,1)}, u32[]{:S(2)}) %copy-start.1) | copy-done | bytes 8388632
  134.4 3.3 %shard_map.59 = bf16[512,512]{1,0:T(8,128)(2,1)S(1)} custom-call(s32[2]{0:T(128)S(1)} %pad_add_fusion.place, bf16[1024,1024]{1,0:T(8,128)(2,1)S(1)} %bitcast.19, bf16[1024,1024]{1,0:T(8,128)(2,1)S(1)} %collective-permute-done.28.b_ref, bf16[1024,4096]{1,0:T(8,128)(2,1)S(1)} %copy-done.1, bf16[4,1024,512]{2,1,0:T(8,128)(2,1)} %collective-permute-done.29.wb_ref), custom_call_target="tpu_custom_call" | custom-call | flops 1073741824 | bytes 6291456 | tf_op jit(solution)/shard_map/pallas_call | solution.py:235
  139.1 3.3 %shard_map.60 = bf16[512,512]{1,0:T(8,128)(2,1)S(1)} custom-call(s32[2]{0:T(128)S(1)} %pad_add_fusion.place, bf16[1024,1024]{1,0:T(8,128)(2,1)S(1)} %bitcast.20, bf16[1024,1024]{1,0:T(8,128)(2,1)S(1)} %collective-permute-done.28.b_ref, bf16[1024,4096]{1,0:T(8,128)(2,1)S(1)} %copy-done.1, bf16[4,1024,512]{2,1,0:T(8,128)(2,1)} %collective-permute-done.29.wb_ref), custom_call_target="tpu_custom_call" | custom-call | flops 1073741824 | bytes 6291456 | tf_op jit(solution)/shard_map/pallas_call | solution.py:235
  144.0 3.3 %shard_map.64 = bf16[512,512]{1,0:T(8,128)(2,1)S(1)} custom-call(s32[2]{0:T(128)S(1)} %pad_add_fusion.place, bf16[1024,1024]{1,0:T(8,128)(2,1)S(1)} %bitcast.21, bf16[1024,1024]{1,0:T(8,128)(2,1)S(1)} %collective-permute-done.28.b_ref, bf16[1024,4096]{1,0:T(8,128)(2,1)S(1)} %copy-done.1, bf16[4,1024,512]{2,1,0:T(8,128)(2,1)} %collective-permute-done.29.wb_ref), custom_call_target="tpu_custom_call" | custom-call | flops 1073741824 | bytes 6291456 | tf_op jit(solution)/shard_map/pallas_call | solution.py:235
  148.9 3.3 %shard_map.62 = bf16[512,512]{1,0:T(8,128)(2,1)S(1)} custom-call(s32[2]{0:T(128)S(1)} %pad_add_fusion.place, bf16[1024,1024]{1,0:T(8,128)(2,1)S(1)} %bitcast.22, bf16[1024,1024]{1,0:T(8,128)(2,1)S(1)} %collective-permute-done.28.b_ref, bf16[1024,4096]{1,0:T(8,128)(2,1)S(1)} %copy-done.1, bf16[4,1024,512]{2,1,0:T(8,128)(2,1)} %collective-permute-done.29.wb_ref), custom_call_target="tpu_custom_call" | custom-call | flops 1073741824 | bytes 6291456 | tf_op jit(solution)/shard_map/pallas_call | solution.py:235
  152.3 3.3 %shard_map.58 = bf16[512,512]{1,0:T(8,128)(2,1)S(1)} custom-call(s32[2]{0:T(128)S(1)} %pad_add_fusion.place, bf16[1024,1024]{1,0:T(8,128)(2,1)S(1)} %bitcast.23, bf16[1024,1024]{1,0:T(8,128)(2,1)S(1)} %collective-permute-done.28.b_ref, bf16[1024,4096]{1,0:T(8,128)(2,1)S(1)} %copy-done.1, bf16[4,1024,512]{2,1,0:T(8,128)(2,1)} %collective-permute-done.29.wb_ref), custom_call_target="tpu_custom_call" | custom-call | flops 1073741824 | bytes 6291456 | tf_op jit(solution)/shard_map/pallas_call | solution.py:235
  155.9 3.3 %shard_map.63 = bf16[512,512]{1,0:T(8,128)(2,1)S(1)} custom-call(s32[2]{0:T(128)S(1)} %pad_add_fusion.place, bf16[1024,1024]{1,0:T(8,128)(2,1)S(1)} %bitcast.24, bf16[1024,1024]{1,0:T(8,128)(2,1)S(1)} %collective-permute-done.28.b_ref, bf16[1024,4096]{1,0:T(8,128)(2,1)S(1)} %copy-done.1, bf16[4,1024,512]{2,1,0:T(8,128)(2,1)} %collective-permute-done.29.wb_ref), custom_call_target="tpu_custom_call" | custom-call | flops 1073741824 | bytes 6291456 | tf_op jit(solution)/shard_map/pallas_call | solution.py:235
  159.2 7.4 %collective-permute-done.34 = bf16[512,512]{1,0:T(8,128)(2,1)S(1)} collective-permute-done((bf16[512,512]{1,0:T(8,128)(2,1)S(1)}, bf16[512,512]{1,0:T(8,128)(2,1)S(1)}, u32[]{:S(2)}, u32[]{:S(2)}) %collective-permute-start.34) | collective-permute-done | bytes 524320 | tf_op jit(solution)/shard_map/ppermute | solution.py:33
  166.7 2.8 %collective-permute-start.35 = (bf16[512,512]{1,0:T(8,128)(2,1)S(1)}, bf16[512,512]{1,0:T(8,128)(2,1)S(1)}, u32[]{:S(2)}, u32[]{:S(2)}) collective-permute-start(bf16[512,512]{1,0:T(8,128)(2,1)S(1)} %add_convert_fusion.1), channel_id=1, source_target_pairs={{0,6},{1,7},{2,0},{3,1},{4,2},{5,3},{6,4},{7,5},{8,14},{9,15},{10,... | collective-permute-start | bytes 1572872 | tf_op jit(solution)/shard_map/ppermute | solution.py:33
  169.6 3.3 %shard_map.61 = bf16[512,512]{1,0:T(8,128)(2,1)S(1)} custom-call(s32[2]{0:T(128)S(1)} %pad_add_fusion.place, bf16[1024,1024]{1,0:T(8,128)(2,1)S(1)} %bitcast.25, bf16[1024,1024]{1,0:T(8,128)(2,1)S(1)} %collective-permute-done.28.b_ref, bf16[1024,4096]{1,0:T(8,128)(2,1)S(1)} %copy-done.1, bf16[4,1024,512]{2,1,0:T(8,128)(2,1)} %collective-permute-done.29.wb_ref), custom_call_target="tpu_custom_call" | custom-call | flops 1073741824 | bytes 6291456 | tf_op jit(solution)/shard_map/pallas_call | solution.py:235
  172.9 3.3 %shard_map.57 = bf16[512,512]{1,0:T(8,128)(2,1)S(1)} custom-call(s32[2]{0:T(128)S(1)} %pad_add_fusion.place, bf16[1024,1024]{1,0:T(8,128)(2,1)S(1)} %bitcast.26, bf16[1024,1024]{1,0:T(8,128)(2,1)S(1)} %collective-permute-done.28.b_ref, bf16[1024,4096]{1,0:T(8,128)(2,1)S(1)} %copy-done.1, bf16[4,1024,512]{2,1,0:T(8,128)(2,1)} %collective-permute-done.29.wb_ref), custom_call_target="tpu_custom_call" | custom-call | flops 1073741824 | bytes 6291456 | tf_op jit(solution)/shard_map/pallas_call | solution.py:235
  177.2 2.2 %collective-permute-done.35 = bf16[512,512]{1,0:T(8,128)(2,1)S(1)} collective-permute-done((bf16[512,512]{1,0:T(8,128)(2,1)S(1)}, bf16[512,512]{1,0:T(8,128)(2,1)S(1)}, u32[]{:S(2)}, u32[]{:S(2)}) %collective-permute-start.35) | collective-permute-done | bytes 524320 | tf_op jit(solution)/shard_map/ppermute | solution.py:33
  (134 shorter events, 46.8 us)
Async XLA Ops:
  0.0 17.4 %collective-permute-start.1 = (bf16[2,512,128]{2,1,0:T(8,128)(2,1)}, bf16[2,512,128]{2,1,0:T(8,128)(2,1)S(1)}, u32[]{:S(2)}, u32[]{:S(2)}) collective-permute-start(bf16[2,512,128]{2,1,0:T(8,128)(2,1)} %bitcast.27), channel_id=1, source_target_pairs={{0,64},{8,72},{16,80},{24,88},{32,96},{40,104},{48,112},{56,120},{... | collective-permute-start | bytes 786440 | tf_op jit(solution)/shard_map/ppermute | solution.py:28
  2.0 15.5 %collective-permute-start.5 = (bf16[2,512,128]{2,1,0:T(8,128)(2,1)}, bf16[2,512,128]{2,1,0:T(8,128)(2,1)S(1)}, u32[]{:S(2)}, u32[]{:S(2)}) collective-permute-start(bf16[2,512,128]{2,1,0:T(8,128)(2,1)} %bitcast.28), channel_id=1, source_target_pairs={{0,8},{8,16},{16,24},{24,32},{32,40},{40,48},{48,56},{56,0},{64,72... | collective-permute-start | bytes 786440 | tf_op jit(solution)/shard_map/ppermute | solution.py:28
  3.7 13.9 %collective-permute-start.4 = (bf16[2,512,128]{2,1,0:T(8,128)(2,1)}, bf16[2,512,128]{2,1,0:T(8,128)(2,1)S(1)}, u32[]{:S(2)}, u32[]{:S(2)}) collective-permute-start(bf16[2,512,128]{2,1,0:T(8,128)(2,1)} %bitcast.29), channel_id=1, source_target_pairs={{0,56},{8,0},{16,8},{24,16},{32,24},{40,32},{48,40},{56,48},{64,12... | collective-permute-start | bytes 786440 | tf_op jit(solution)/shard_map/ppermute | solution.py:28
  7.6 12.7 %collective-permute-start = (bf16[2,512,128]{2,1,0:T(8,128)(2,1)}, bf16[2,512,128]{2,1,0:T(8,128)(2,1)S(1)}, u32[]{:S(2)}, u32[]{:S(2)}) collective-permute-start(bf16[2,512,128]{2,1,0:T(8,128)(2,1)} %bitcast.30), channel_id=1, source_target_pairs={{0,192},{8,200},{16,208},{24,216},{32,224},{40,232},{48,240},{56,2... | collective-permute-start | bytes 786440 | tf_op jit(solution)/shard_map/ppermute | solution.py:28
  15.9 115.2 %collective-permute-start.29 = (bf16[4,1024,512]{2,1,0:T(8,128)(2,1)}, bf16[4,1024,512]{2,1,0:T(8,128)(2,1)}, u32[]{:S(2)}, u32[]{:S(2)}) collective-permute-start(bf16[4,1024,512]{2,1,0:T(8,128)(2,1)} %shard_map.56), channel_id=1, source_target_pairs={{0,1},{1,0},{2,3},{3,2},{4,5},{5,4},{6,7},{7,6},{8,9},{9,8},{10,11... | collective-permute-start | bytes 12582920 | tf_op jit(solution)/shard_map/ppermute | solution.py:37
  17.4 6.4 %collective-permute-start.3 = (bf16[1,512,128]{2,1,0:T(8,128)(2,1)S(1)}, bf16[1,512,128]{2,1,0:T(8,128)(2,1)S(1)}, u32[]{:S(2)}, u32[]{:S(2)}) collective-permute-start(bf16[1,512,128]{2,1,0:T(8,128)(2,1)S(1)} %slice.67), channel_id=1, source_target_pairs={{0,64},{8,72},{16,80},{24,88},{32,96},{40,104},{48,112},{56,120},{... | collective-permute-start | bytes 393224 | tf_op jit(solution)/shard_map/ppermute | solution.py:28
  17.5 9.0 %collective-permute-start.7 = (bf16[2,512,128]{2,1,0:T(8,128)(2,1)S(1)}, bf16[2,512,128]{2,1,0:T(8,128)(2,1)S(1)}, u32[]{:S(2)}, u32[]{:S(2)}) collective-permute-start(bf16[2,512,128]{2,1,0:T(8,128)(2,1)S(1)} %collective-permute-done.5.rest_6_), channel_id=1, source_target_pairs={{0,8},{8,16},{16,24},{24,32},{32,40},{40,48},{48,56},{56,0},{64,72... | collective-permute-start | bytes 786440 | tf_op jit(solution)/shard_map/ppermute | solution.py:28
  17.6 8.9 %collective-permute-start.6 = (bf16[2,512,128]{2,1,0:T(8,128)(2,1)S(1)}, bf16[2,512,128]{2,1,0:T(8,128)(2,1)S(1)}, u32[]{:S(2)}, u32[]{:S(2)}) collective-permute-start(bf16[2,512,128]{2,1,0:T(8,128)(2,1)S(1)} %collective-permute-done.4.rest_5_), channel_id=1, source_target_pairs={{0,56},{8,0},{16,8},{24,16},{32,24},{40,32},{48,40},{56,48},{64,12... | collective-permute-start | bytes 786440 | tf_op jit(solution)/shard_map/ppermute | solution.py:28
  23.9 19.5 %collective-permute-start.13 = (bf16[3,512,128]{2,1,0:T(8,128)(2,1)S(1)}, bf16[3,512,128]{2,1,0:T(8,128)(2,1)S(1)}, u32[]{:S(2)}, u32[]{:S(2)}) collective-permute-start(bf16[3,512,128]{2,1,0:T(8,128)(2,1)S(1)} %pad_maximum_fusion.2), channel_id=1, source_target_pairs={{0,8},{8,16},{16,24},{24,32},{32,40},{40,48},{48,56},{56,0},{64,72... | collective-permute-start | bytes 1179656 | tf_op jit(solution)/shard_map/ppermute | solution.py:28
  26.5 14.1 %collective-permute-start.9 = (bf16[2,512,128]{2,1,0:T(8,128)(2,1)S(1)}, bf16[2,512,128]{2,1,0:T(8,128)(2,1)S(1)}, u32[]{:S(2)}, u32[]{:S(2)}) collective-permute-start(bf16[2,512,128]{2,1,0:T(8,128)(2,1)S(1)} %collective-permute-done.7.rest_8_), channel_id=1, source_target_pairs={{0,8},{8,16},{16,24},{24,32},{32,40},{40,48},{48,56},{56,0},{64,72... | collective-permute-start | bytes 786440 | tf_op jit(solution)/shard_map/ppermute | solution.py:28
  26.6 15.0 %collective-permute-start.8 = (bf16[2,512,128]{2,1,0:T(8,128)(2,1)S(1)}, bf16[2,512,128]{2,1,0:T(8,128)(2,1)S(1)}, u32[]{:S(2)}, u32[]{:S(2)}) collective-permute-start(bf16[2,512,128]{2,1,0:T(8,128)(2,1)S(1)} %collective-permute-done.6.rest_7_), channel_id=1, source_target_pairs={{0,56},{8,0},{16,8},{24,16},{32,24},{40,32},{48,40},{56,48},{64,12... | collective-permute-start | bytes 786440 | tf_op jit(solution)/shard_map/ppermute | solution.py:28
  29.2 14.8 %collective-permute-start.12 = (bf16[3,512,128]{2,1,0:T(8,128)(2,1)S(1)}, bf16[3,512,128]{2,1,0:T(8,128)(2,1)S(1)}, u32[]{:S(2)}, u32[]{:S(2)}) collective-permute-start(bf16[3,512,128]{2,1,0:T(8,128)(2,1)S(1)} %pad_maximum_fusion.2), channel_id=1, source_target_pairs={{0,56},{8,0},{16,8},{24,16},{32,24},{40,32},{48,40},{56,48},{64,12... | collective-permute-start | bytes 1179656 | tf_op jit(solution)/shard_map/ppermute | solution.py:28
  40.6 12.9 %collective-permute-start.21 = (bf16[4,512,128]{2,1,0:T(8,128)(2,1)S(1)}, bf16[4,512,128]{2,1,0:T(8,128)(2,1)S(1)}, u32[]{:S(2)}, u32[]{:S(2)}) collective-permute-start(bf16[4,512,128]{2,1,0:T(8,128)(2,1)S(1)} %pad_maximum_fusion.1), channel_id=1, source_target_pairs={{0,64},{8,72},{16,80},{24,88},{32,96},{40,104},{48,112},{56,120},{... | collective-permute-start | bytes 1572872 | tf_op jit(solution)/shard_map/ppermute | solution.py:28
  41.6 12.3 %collective-permute-start.20 = (bf16[4,512,128]{2,1,0:T(8,128)(2,1)S(1)}, bf16[4,512,128]{2,1,0:T(8,128)(2,1)S(1)}, u32[]{:S(2)}, u32[]{:S(2)}) collective-permute-start(bf16[4,512,128]{2,1,0:T(8,128)(2,1)S(1)} %pad_maximum_fusion.1), channel_id=1, source_target_pairs={{0,192},{8,200},{16,208},{24,216},{32,224},{40,232},{48,240},{56,2... | collective-permute-start | bytes 1572872 | tf_op jit(solution)/shard_map/ppermute | solution.py:28
  44.0 12.2 %collective-permute-start.15 = (bf16[3,512,128]{2,1,0:T(8,128)(2,1)S(1)}, bf16[3,512,128]{2,1,0:T(8,128)(2,1)S(1)}, u32[]{:S(2)}, u32[]{:S(2)}) collective-permute-start(bf16[3,512,128]{2,1,0:T(8,128)(2,1)S(1)} %collective-permute-done.13.rest_14_), channel_id=1, source_target_pairs={{0,8},{8,16},{16,24},{24,32},{32,40},{40,48},{48,56},{56,0},{64,72... | collective-permute-start | bytes 1179656 | tf_op jit(solution)/shard_map/ppermute | solution.py:28
  47.6 9.5 %collective-permute-start.14 = (bf16[3,512,128]{2,1,0:T(8,128)(2,1)S(1)}, bf16[3,512,128]{2,1,0:T(8,128)(2,1)S(1)}, u32[]{:S(2)}, u32[]{:S(2)}) collective-permute-start(bf16[3,512,128]{2,1,0:T(8,128)(2,1)S(1)} %collective-permute-done.12.rest_13_), channel_id=1, source_target_pairs={{0,56},{8,0},{16,8},{24,16},{32,24},{40,32},{48,40},{56,48},{64,12... | collective-permute-start | bytes 1179656 | tf_op jit(solution)/shard_map/ppermute | solution.py:28
  53.6 9.3 %collective-permute-start.25 = (bf16[3,512,128]{2,1,0:T(8,128)(2,1)S(1)}, bf16[3,512,128]{2,1,0:T(8,128)(2,1)}, u32[]{:S(2)}, u32[]{:S(2)}) collective-permute-start(bf16[3,512,128]{2,1,0:T(8,128)(2,1)S(1)} %pad_maximum_fusion.3), channel_id=1, source_target_pairs={{0,64},{8,72},{16,80},{24,88},{32,96},{40,104},{48,112},{56,120},{... | collective-permute-start | bytes 1179656 | tf_op jit(solution)/shard_map/ppermute | solution.py:28
  53.9 9.0 %collective-permute-start.24 = (bf16[3,512,128]{2,1,0:T(8,128)(2,1)S(1)}, bf16[3,512,128]{2,1,0:T(8,128)(2,1)}, u32[]{:S(2)}, u32[]{:S(2)}) collective-permute-start(bf16[3,512,128]{2,1,0:T(8,128)(2,1)S(1)} %pad_maximum_fusion.3), channel_id=1, source_target_pairs={{0,192},{8,200},{16,208},{24,216},{32,224},{40,232},{48,240},{56,2... | collective-permute-start | bytes 1179656 | tf_op jit(solution)/shard_map/ppermute | solution.py:28
  56.3 9.3 %collective-permute-start.17 = (bf16[3,512,128]{2,1,0:T(8,128)(2,1)S(1)}, bf16[3,512,128]{2,1,0:T(8,128)(2,1)}, u32[]{:S(2)}, u32[]{:S(2)}) collective-permute-start(bf16[3,512,128]{2,1,0:T(8,128)(2,1)S(1)} %collective-permute-done.15.rest_16_), channel_id=1, source_target_pairs={{0,8},{8,16},{16,24},{24,32},{32,40},{40,48},{48,56},{56,0},{64,72... | collective-permute-start | bytes 1179656 | tf_op jit(solution)/shard_map/ppermute | solution.py:28
  57.1 9.1 %collective-permute-start.16 = (bf16[3,512,128]{2,1,0:T(8,128)(2,1)S(1)}, bf16[3,512,128]{2,1,0:T(8,128)(2,1)}, u32[]{:S(2)}, u32[]{:S(2)}) collective-permute-start(bf16[3,512,128]{2,1,0:T(8,128)(2,1)S(1)} %collective-permute-done.14.rest_15_), channel_id=1, source_target_pairs={{0,56},{8,0},{16,8},{24,16},{32,24},{40,32},{48,40},{56,48},{64,12... | collective-permute-start | bytes 1179656 | tf_op jit(solution)/shard_map/ppermute | solution.py:28
  62.9 10.8 %collective-permute-start.23 = (bf16[2,512,128]{2,1,0:T(8,128)(2,1)}, bf16[2,512,128]{2,1,0:T(8,128)(2,1)}, u32[]{:S(2)}, u32[]{:S(2)}) collective-permute-start(bf16[2,512,128]{2,1,0:T(8,128)(2,1)} %slice.78), channel_id=1, source_target_pairs={{0,64},{8,72},{16,80},{24,88},{32,96},{40,104},{48,112},{56,120},{... | collective-permute-start | bytes 786440 | tf_op jit(solution)/shard_map/ppermute | solution.py:28
  62.9 12.8 %collective-permute-start.22 = (bf16[2,512,128]{2,1,0:T(8,128)(2,1)}, bf16[2,512,128]{2,1,0:T(8,128)(2,1)}, u32[]{:S(2)}, u32[]{:S(2)}) collective-permute-start(bf16[2,512,128]{2,1,0:T(8,128)(2,1)} %slice.77), channel_id=1, source_target_pairs={{0,192},{8,200},{16,208},{24,216},{32,224},{40,232},{48,240},{56,2... | collective-permute-start | bytes 786440 | tf_op jit(solution)/shard_map/ppermute | solution.py:28
  70.6 6.2 %collective-permute-start.27 = (bf16[3,256,128]{2,1,0:T(8,128)(2,1)S(1)}, bf16[3,256,128]{2,1,0:T(8,128)(2,1)S(1)}, u32[]{:S(2)}, u32[]{:S(2)}) collective-permute-start(bf16[3,256,128]{2,1,0:T(8,128)(2,1)S(1)} %slice.81), channel_id=1, source_target_pairs={{0,64},{8,72},{16,80},{24,88},{32,96},{40,104},{48,112},{56,120},{... | collective-permute-start | bytes 589832 | tf_op jit(solution)/shard_map/ppermute | solution.py:28
  73.7 5.7 %collective-permute-start.19 = (bf16[3,256,128]{2,1,0:T(8,128)(2,1)S(1)}, bf16[3,256,128]{2,1,0:T(8,128)(2,1)S(1)}, u32[]{:S(2)}, u32[]{:S(2)}) collective-permute-start(bf16[3,256,128]{2,1,0:T(8,128)(2,1)S(1)} %slice.72), channel_id=1, source_target_pairs={{0,8},{8,16},{16,24},{24,32},{32,40},{40,48},{48,56},{56,0},{64,72... | collective-permute-start | bytes 589832 | tf_op jit(solution)/shard_map/ppermute | solution.py:28
  75.7 5.7 %collective-permute-start.18 = (bf16[3,256,128]{2,1,0:T(8,128)(2,1)S(1)}, bf16[3,256,128]{2,1,0:T(8,128)(2,1)S(1)}, u32[]{:S(2)}, u32[]{:S(2)}) collective-permute-start(bf16[3,256,128]{2,1,0:T(8,128)(2,1)S(1)} %slice.71), channel_id=1, source_target_pairs={{0,56},{8,0},{16,8},{24,16},{32,24},{40,32},{48,40},{56,48},{64,12... | collective-permute-start | bytes 589832 | tf_op jit(solution)/shard_map/ppermute | solution.py:28
  121.6 9.5 %collective-permute-start.28 = (bf16[1024,1024]{1,0:T(8,128)(2,1)S(1)}, bf16[1024,1024]{1,0:T(8,128)(2,1)S(1)}, u32[]{:S(2)}, u32[]{:S(2)}) collective-permute-start(bf16[1024,1024]{1,0:T(8,128)(2,1)S(1)} %bitcast.18), channel_id=1, source_target_pairs={{0,1},{1,0},{2,3},{3,2},{4,5},{5,4},{6,7},{7,6},{8,9},{9,8},{10,11... | collective-permute-start | bytes 6291464 | tf_op jit(solution)/shard_map/ppermute | solution.py:37
  137.7 17.9 %collective-permute-start.30 = (bf16[512,512]{1,0:T(8,128)(2,1)S(1)}, bf16[512,512]{1,0:T(8,128)(2,1)S(1)}, u32[]{:S(2)}, u32[]{:S(2)}) collective-permute-start(bf16[512,512]{1,0:T(8,128)(2,1)S(1)} %shard_map.59), channel_id=1, source_target_pairs={{0,2},{1,3},{2,4},{3,5},{4,6},{5,7},{6,0},{7,1},{8,10},{9,11},{10,... | collective-permute-start | bytes 1572872 | tf_op jit(solution)/shard_map/ppermute | solution.py:33
  142.5 33.8 %collective-permute-start.32 = (bf16[512,512]{1,0:T(8,128)(2,1)S(1)}, bf16[512,512]{1,0:T(8,128)(2,1)S(1)}, u32[]{:S(2)}, u32[]{:S(2)}) collective-permute-start(bf16[512,512]{1,0:T(8,128)(2,1)S(1)} %shard_map.60), channel_id=1, source_target_pairs={{0,6},{1,7},{2,0},{3,1},{4,2},{5,3},{6,4},{7,5},{8,14},{9,15},{10,... | collective-permute-start | bytes 1572872 | tf_op jit(solution)/shard_map/ppermute | solution.py:33
  147.3 19.3 %collective-permute-start.34 = (bf16[512,512]{1,0:T(8,128)(2,1)S(1)}, bf16[512,512]{1,0:T(8,128)(2,1)S(1)}, u32[]{:S(2)}, u32[]{:S(2)}) collective-permute-start(bf16[512,512]{1,0:T(8,128)(2,1)S(1)} %shard_map.64), channel_id=1, source_target_pairs={{0,6},{1,7},{2,0},{3,1},{4,2},{5,3},{6,4},{7,5},{8,14},{9,15},{10,... | collective-permute-start | bytes 1572872 | tf_op jit(solution)/shard_map/ppermute | solution.py:33
  152.2 24.9 %collective-permute-start.33 = (bf16[512,512]{1,0:T(8,128)(2,1)S(1)}, bf16[512,512]{1,0:T(8,128)(2,1)S(1)}, u32[]{:S(2)}, u32[]{:S(2)}) collective-permute-start(bf16[512,512]{1,0:T(8,128)(2,1)S(1)} %shard_map.62), channel_id=1, source_target_pairs={{0,2},{1,3},{2,4},{3,5},{4,6},{5,7},{6,0},{7,1},{8,10},{9,11},{10,... | collective-permute-start | bytes 1572872 | tf_op jit(solution)/shard_map/ppermute | solution.py:33
  155.8 21.1 %collective-permute-start.31 = (bf16[512,512]{1,0:T(8,128)(2,1)S(1)}, bf16[512,512]{1,0:T(8,128)(2,1)S(1)}, u32[]{:S(2)}, u32[]{:S(2)}) collective-permute-start(bf16[512,512]{1,0:T(8,128)(2,1)S(1)} %add_convert_fusion.3), channel_id=1, source_target_pairs={{0,2},{1,3},{2,4},{3,5},{4,6},{5,7},{6,0},{7,1},{8,10},{9,11},{10,... | collective-permute-start | bytes 1572872 | tf_op jit(solution)/shard_map/ppermute | solution.py:33
  166.7 12.6 %collective-permute-start.35 = (bf16[512,512]{1,0:T(8,128)(2,1)S(1)}, bf16[512,512]{1,0:T(8,128)(2,1)S(1)}, u32[]{:S(2)}, u32[]{:S(2)}) collective-permute-start(bf16[512,512]{1,0:T(8,128)(2,1)S(1)} %add_convert_fusion.1), channel_id=1, source_target_pairs={{0,6},{1,7},{2,0},{3,1},{4,2},{5,3},{6,4},{7,5},{8,14},{9,15},{10,... | collective-permute-start | bytes 1572872 | tf_op jit(solution)/shard_map/ppermute | solution.py:33
  (34 other events, 264.5 us)

commit v2 on v1

v2 whole, which is shorter than its diff:
```python
import functools
import math

import jax
import jax.numpy as jnp
from jax import lax
from jax.experimental import pallas as pl
from jax.experimental.pallas import tpu as pltpu
from jax.sharding import PartitionSpec as P

H = 64
KVH = 8
HD = 128
GROUP = H // KVH
NX = 4
NZ = 8
NY = 4
LOG2E = 1.4426950408889634
MIB = 1024 * 1024


def send_cache(value, step_x, step_z):
    pairs = [
        (x * NZ + z, ((x + step_x) % NX) * NZ + (z + step_z) % NZ)
        for x in range(NX)
        for z in range(NZ)
    ]
    return lax.ppermute(value, "cache", pairs)


def send_y(value, step):
    pairs = [(2 * y + c, 2 * ((y + step) % NY) + c) for y in range(NY) for c in range(2)]
    return lax.ppermute(value, "tensor", pairs)


def swap_core(value):
    return lax.ppermute(value, "tensor", [(t, t ^ 1) for t in range(2 * NY)])


def together(*values):
    return lax.optimization_barrier(values)


def gather_prefix(block):
    pieces = []
    length = block.shape[1]
    half = length // 2

    def whole(array, dz, dx):
        for kv in range(2):
            part(array, kv, kv, dz, dx)

    def part(array, at, kv, dz, dx, first=0):
        pieces.append((array, at, kv, (dz % NZ) * NX + dx % NX, first))

    whole(block, 0, 0)
    z1a, z1b = send_cache(block, 0, -1), send_cache(block, 0, 1)
    x1a, x1b = send_cache(block, -1, 0), send_cache(block, 1, 0)
    z1a, z1b, x1a, x1b = together(z1a, z1b, x1a, x1b)
    z2a, z2b = send_cache(z1a, 0, -1), send_cache(z1b, 0, 1)
    key_x2, value_x2 = send_cache(x1a[0:1], -1, 0), send_cache(x1b[1:2], 1, 0)
    z2a, z2b, key_x2, value_x2 = together(z2a, z2b, key_x2, value_x2)
    z3a, z3b = send_cache(z2a, 0, -1), send_cache(z2b, 0, 1)
    near = jnp.concatenate([z1a[0:1], z1b[0:1], z2a[0:1], z2b[0:1]], axis=0)
    near_a, near_b = send_cache(near, -1, 0), send_cache(near, 1, 0)
    values = jnp.concatenate([x1a[1:2], x1b[1:2], value_x2], axis=0)
    v1a, v1b = send_cache(values, 0, -1), send_cache(values, 0, 1)
    z3a, z3b, near_a, near_b, v1a, v1b = together(z3a, z3b, near_a, near_b, v1a, v1b)
    key_z4, value_z4 = send_cache(z3a[0:1], 0, -1), send_cache(z3b[1:2], 0, 1)
    near_c, near_d = send_cache(near_a[:2], -1, 0), send_cache(near_b[2:], 1, 0)
    v2a, v2b = send_cache(v1a, 0, -1), send_cache(v1b, 0, 1)
    key_z4, value_z4, near_c, near_d, v2a, v2b = together(
        key_z4, value_z4, near_c, near_d, v2a, v2b
    )
    v3a, v3b = send_cache(v2a, 0, -1), send_cache(v2b, 0, 1)
    distant = jnp.concatenate([z3a[0:1], z3b[0:1], key_z4], axis=0)
    far_a, far_b = send_cache(distant, -1, 0), send_cache(distant, 1, 0)
    v3a, v3b, far_a, far_b = together(v3a, v3b, far_a, far_b)
    v4a, v4b = send_cache(v3a[:, :half], 0, -1), send_cache(v3b[:, half:], 0, 1)
    far_c, far_d = send_cache(far_a[:, :half], -1, 0), send_cache(far_b[:, half:], 1, 0)

    for step, ahead, behind in ((1, z1a, z1b), (2, z2a, z2b), (3, z3a, z3b)):
        whole(ahead, step, 0)
        whole(behind, -step, 0)
    part(key_z4, 0, 0, 4, 0)
    part(value_z4, 0, 1, 4, 0)
    whole(x1a, 0, 1)
    whole(x1b, 0, -1)
    part(key_x2, 0, 0, 0, 2)
    part(value_x2, 0, 1, 0, 2)
    for at, dx in enumerate((1, -1, 2)):
        for step, ahead, behind in ((1, v1a, v1b), (2, v2a, v2b), (3, v3a, v3b)):
            part(ahead, at, 1, step, dx)
            part(behind, at, 1, -step, dx)
        part(v4a, at, 1, 4, dx, 0)
        part(v4b, at, 1, 4, dx, half)
    for at, dz in enumerate((1, -1, 2, -2)):
        part(near_a, at, 0, dz, 1)
        part(near_b, at, 0, dz, -1)
        part(near_c if at < 2 else near_d, at % 2, 0, dz, 2)
    for at, dz in enumerate((3, -3, 4)):
        part(far_a, at, 0, dz, 1)
        part(far_b, at, 0, dz, -1)
        part(far_c, at, 0, dz, 2, 0)
        part(far_d, at, 0, dz, 2, half)
    return pieces


LAST = (((1,), (1,)), ((), ()))
INNER = (((1,), (0,)), ((), ()))


def beside_ones(values):
    return jnp.concatenate([values, jnp.ones_like(values)], axis=1)


def attention_kernel(places, n_arrays, batch, codes, q_ref, s_ref, *rest):
    arrays = rest[:n_arrays]
    o_ref, cache, sems = rest[n_arrays:]
    count, suffix, _ = q_ref.shape
    rows = GROUP * suffix
    factor = LOG2E / math.sqrt(HD)

    def copies():
        for n, (which, at, kv, code, first) in enumerate(places):
            yield pltpu.make_async_copy(
                arrays[which].at[at],
                cache.at[kv, code, pl.ds(first, arrays[which].shape[1])],
                sems.at[n],
            )

    for copy in copies():
        copy.start()
    for copy in copies():
        copy.wait()

    token = lax.broadcasted_iota(jnp.int32, (rows, HD), 0) % suffix
    causal = lax.broadcasted_iota(jnp.int32, (rows, HD), 1) <= token
    blank = jnp.zeros((HD - suffix, HD), jnp.bfloat16)

    @pl.loop(0, count // batch)
    def _(step):
        scores = []
        for i in range(batch):
            n = step * batch + i
            q = jnp.concatenate([q_ref[n, :, g * HD : (g + 1) * HD] for g in range(GROUP)], axis=0)
            far = lax.dot_general(
                q, cache[0, codes[n]], LAST, preferred_element_type=jnp.float32
            )
            keys = jnp.concatenate([s_ref[0, n], blank], axis=0)
            near = lax.dot_general(q, keys, LAST, preferred_element_type=jnp.float32)
            near = jnp.where(causal, near, -jnp.inf)
            tiles = [far[:, j : j + HD] for j in range(0, far.shape[1], HD)]
            scores.append(tiles + [near])
        weights = []
        for tiles in scores:
            top = jnp.max(functools.reduce(jnp.maximum, tiles), axis=1, keepdims=True)
            weights.append([jnp.exp2((s - top) * factor).astype(jnp.bfloat16) for s in tiles])
        for i in range(batch):
            n = step * batch + i
            far = jnp.concatenate(weights[i][:-1], axis=1)
            near = weights[i][-1][:, :suffix]
            summed = lax.dot_general(
                far, beside_ones(cache[1, codes[n]]), INNER, preferred_element_type=jnp.float32
            ) + lax.dot_general(
                near, beside_ones(s_ref[1, n]), INNER, preferred_element_type=jnp.float32
            )
            out = (summed[:, :HD] / summed[:, HD:]).astype(jnp.bfloat16)
            for g in range(GROUP):
                o_ref[n, :, g * HD : (g + 1) * HD] = out[g * suffix : (g + 1) * suffix]


def attend(codes, queries, suffix_kv, pieces, length):
    arrays = []
    places = []
    for array, at, kv, code, first in pieces:
        which = next((n for n, a in enumerate(arrays) if a is array), len(arrays))
        if which == len(arrays):
            arrays.append(array)
        places.append((which, at, kv, code, first))
    count, suffix, width = queries.shape
    vmem = pl.BlockSpec(memory_space=pltpu.VMEM)
    return pl.pallas_call(
        functools.partial(attention_kernel, places, len(arrays), 4),
        out_shape=jax.ShapeDtypeStruct(queries.shape, jnp.bfloat16),
        in_specs=[pl.BlockSpec(memory_space=pltpu.SMEM), vmem, vmem]
        + [pl.BlockSpec(memory_space=pl.ANY)] * len(arrays),
        out_specs=vmem,
        scratch_shapes=[
            pltpu.VMEM((2, NX * NZ, length, HD), jnp.bfloat16),
            pltpu.SemaphoreType.DMA((len(places),)),
        ],
        compiler_params=pltpu.CompilerParams(vmem_limit_bytes=24 * MIB),
        cost_estimate=pl.CostEstimate(
            flops=4 * count * suffix * width * length,
            bytes_accessed=16 * MIB,
            transcendentals=count * suffix * GROUP * length,
        ),
    )(codes, queries, suffix_kv, *arrays)


def pick_kernel(place, w_ref, o_ref, sems):
    width = o_ref.shape[2]
    copies = [
        pltpu.make_async_copy(
            w_ref.at[:, pl.ds(pl.multiple_of((2 * n + 1 - place[1]) * width, width), width)],
            o_ref.at[n],
            sems.at[n],
        )
        for n in range(NY)
    ]
    for copy in copies:
        copy.start()
    for copy in copies:
        copy.wait()


def pick_columns(place, w_out, width):
    hbm = pl.BlockSpec(memory_space=pltpu.HBM)
    return pl.pallas_call(
        pick_kernel,
        out_shape=jax.ShapeDtypeStruct((NY, w_out.shape[0], width), w_out.dtype),
        in_specs=[pl.BlockSpec(memory_space=pltpu.SMEM), hbm],
        out_specs=hbm,
        scratch_shapes=[pltpu.SemaphoreType.DMA((NY,))],
        cost_estimate=pl.CostEstimate(flops=0, bytes_accessed=8 * MIB, transcendentals=0),
    )(place, w_out)


def project_kernel(tiles, place, a_ref, b_ref, w_ref, m_ref, *outs):
    total = jnp.dot(a_ref[...], w_ref[...], preferred_element_type=jnp.float32)
    total += jnp.dot(b_ref[...], m_ref[0], preferred_element_type=jnp.float32)
    total = total.astype(jnp.bfloat16)
    for at, out in enumerate(outs):

        @pl.when(pl.program_id(0) // tiles == at)
        def _(out=out):
            out[...] = total


def project(place, mine, mate, w_out, w_mate, parts, rows):
    depth, width = w_mate.shape[1:]
    tile = min(256, rows)
    tiles = rows // tile

    def pick(n, choices):
        value = choices[-1]
        for at in range(len(choices) - 2, -1, -1):
            value = jnp.where(n // tiles == at, choices[at], value)
        return value

    def row(n, p):
        return (pick(n, [first // tile for _, first in parts]) + n % tiles, 0)

    def chip(n, p):
        return (p[0] + pick(n, [turn for turn, _ in parts])) % NY

    def out(at):
        return lambda n, p: (jnp.clip(n - at * tiles, 0, tiles - 1), 0)

    hbm = pltpu.HBM
    return pl.pallas_call(
        functools.partial(project_kernel, tiles),
        out_shape=[jax.ShapeDtypeStruct((rows, width), jnp.bfloat16)] * len(parts),
        grid_spec=pltpu.PrefetchScalarGridSpec(
            num_scalar_prefetch=1,
            grid=(tiles * len(parts),),
            in_specs=[
                pl.BlockSpec((tile, depth), row),
                pl.BlockSpec((tile, depth), row),
                pl.BlockSpec((depth, width), lambda n, p: (0, 2 * chip(n, p) + p[1])),
                pl.BlockSpec((1, depth, width), lambda n, p: (chip(n, p), 0, 0)),
            ],
            out_specs=[pl.BlockSpec((tile, width), out(at)) for at in range(len(parts))],
        ),
        compiler_params=pltpu.CompilerParams(vmem_limit_bytes=24 * MIB),
        cost_estimate=pl.CostEstimate(
            flops=4 * rows * len(parts) * depth * width,
            bytes_accessed=6 * MIB,
            transcendentals=0,
        ),
    )(place, mine, mate, w_out, w_mate)


def final_kernel(own, top1, top3, low1, low3, o_ref):
    half = top1.shape[0]
    for first, a, b in ((0, top1, top3), (half, low1, low3)):
        total = own[first : first + half].astype(jnp.float32) + a[...] + b[...]
        o_ref[first : first + half] = total.astype(jnp.bfloat16)


def added(*terms):
    return sum(t.astype(jnp.float32) for t in terms).astype(jnp.bfloat16)


def shards(queries, prefix_kv, suffix_kv, candidate_prefix, w_out):
    count, suffix, width = queries.shape
    length = prefix_kv.shape[2]
    out_width = w_out.shape[1] // (2 * NY)
    me = lax.axis_index("cache")
    t = lax.axis_index("tensor")
    place = jnp.stack([t // 2, t % 2]).astype(jnp.int32)
    ids = candidate_prefix[:, 0]
    codes = ((ids % NZ - me % NZ) % NZ) * NX + (ids // NZ - me // NZ) % NX

    pieces = gather_prefix(prefix_kv.reshape(2, length, HD))
    w_mate = swap_core(pick_columns(place, w_out, out_width))
    mine = attend(codes, queries, suffix_kv, pieces, length).reshape(count * suffix, width)
    mate = swap_core(mine)

    rows = count * suffix
    half = rows // 2
    part = functools.partial(project, place, mine, mate, w_out, w_mate)
    top2, low2 = part([(2, 0), (2, half)], half)
    top2, low2 = send_y(top2, 1), send_y(low2, -1)
    low1, top3 = part([(1, half), (3, 0)], half)
    low1, top3 = send_y(low1, 1), send_y(top3, -1)
    own_top1, own_low3 = part([(1, 0), (3, half)], half)
    top1 = send_y(added(own_top1, top2), 1)
    low3 = send_y(added(own_low3, low2), -1)
    (own,) = part([(0, 0)], rows)
    vmem = pl.BlockSpec(memory_space=pltpu.VMEM)
    out = pl.pallas_call(
        final_kernel,
        out_shape=jax.ShapeDtypeStruct((rows, out_width), jnp.bfloat16),
        in_specs=[vmem] * 5,
        out_specs=vmem,
        compiler_params=pltpu.CompilerParams(vmem_limit_bytes=16 * MIB),
    )(own, top1, top3, low1, low3)
    return out.reshape(count, suffix, out_width)


def solution(mesh):
    in_specs = (
        P("cache", None, "tensor"),
        P(None, "cache", None, "tensor"),
        P(None, "cache", None, "tensor"),
        P("cache", None),
        P("tensor", None),
    )
    out_specs = P("cache", None, "tensor")
    return jax.shard_map(shards, mesh=mesh, in_specs=in_specs, out_specs=out_specs, check_vma=False)
```

time: 183 us -> 310 us (1.69)
  Pallas kernels: 56.6 us -> 169 us
  waiting for transfers between devices: 43.9 us -> 52.4 us
  starting transfers between devices: 50 us -> 57.3 us
    pallas_call x10 -> x7, Pallas kernels: 56.6 us -> 169 us  [the longest x1 129 us: pick_columns(): pl.pallas_call(pick_kernel, out_shape=jax.ShapeDtypeStruct((NY, w_out.sha...]
    ppermute x28, waiting for transfers between devices: 29.9 us -> 35.2 us  [send_cache(): return lax.ppermute(value, 'cache', pairs)]
    ppermute x2, starting transfers between devices: 7.18 us -> 11.2 us  [swap_core(): return lax.ppermute(value, 'tensor', [(t, t ^ 1) for t in range(2 * NY)])]
    ppermute x28, starting transfers between devices: 35.4 us -> 38.8 us  [send_cache(): return lax.ppermute(value, 'cache', pairs)]
    ppermute x6, waiting for transfers between devices: 10.2 us -> 13.4 us  [send_y(): return lax.ppermute(value, 'tensor', pairs)]
    unnamed x60 -> x54, local copies, waits for them, and re-layouts: 21.1 us -> 19 us
  transfers between devices with their start and end apart: 36 -> 36, of which waited for: 15 -> 17; matrix products, arithmetic and copies ran while one was open for 4% -> 4% of each run, Pallas kernels for 29% -> 53%
where the time goes in v2:
time: 310 us; the launch traced here: 309 us
  Pallas kernels  169 us (55%)
  starting transfers between devices  57.3 us (18%)
  waiting for transfers between devices  52.4 us (17%)
  local copies, waits for them, and re-layouts  27.4 us (9%)
    pallas_call x1, Pallas kernels, pick_columns(): pl.pallas_call(pick_kernel, out_shape=jax.ShapeDtypeStruct((NY, w_out.sha...  129 us
    ppermute x28, starting transfers between devices, send_cache(): return lax.ppermute(value, 'cache', pairs)  38.8 us
    ppermute x28, waiting for transfers between devices, send_cache(): return lax.ppermute(value, 'cache', pairs)  35.2 us
    pallas_call x4, Pallas kernels, project(): pl.pallas_call(functools.partial(project_kernel, tiles), out_shape=[jax.S...  21 us
    unnamed x54, local copies, waits for them, and re-layouts  19 us
    pallas_call x1, Pallas kernels, attend(): pl.pallas_call(functools.partial(attention_kernel, places, len(arrays), 4...  17.9 us
    ppermute x6, waiting for transfers between devices, send_y(): return lax.ppermute(value, 'tensor', pairs)  13.4 us
    ppermute x2, starting transfers between devices, swap_core(): return lax.ppermute(value, 'tensor', [(t, t ^ 1) for t in range(2 * NY)])  11.2 us
  transfers between devices with their start and end apart: 36, of which 17 were waited for; matrix products, arithmetic and copies ran while one was open for 4% of the time, Pallas kernels for 53%

profile of v2, /device:TPU:1, one launch (start us, length us, event | category | flops | bytes accessed | tf_op | source)
XLA Modules:
  0.0 309.2 jit_solution(3855951787225521773)
XLA Ops:
  0.0 2.0 collective-permute-start.3
  3.3 1.8 collective-permute-start.1
  5.1 3.9 %collective-permute-start = (bf16[2,512,128]{2,1,0:T(8,128)(2,1)}, bf16[2,512,128]{2,1,0:T(8,128)(2,1)S(1)}, u32[]{:S(2)}, u32[]{:S(2)}) collective-permute-start(bf16[2,512,128]{2,1,0:T(8,128)(2,1)} %bitcast.26), channel_id=1, source_target_pairs={{0,56},{8,0},{16,8},{24,16},{32,24},{40,32},{48,40},{56,48},{64,12... | collective-permute-start | bytes 786440 | tf_op jit(solution)/shard_map/ppermute | solution.py:28
  9.1 5.6 %collective-permute-done.1.rest_2_ = bf16[2,512,128]{2,1,0:T(8,128)(2,1)S(1)} collective-permute-done((bf16[2,512,128]{2,1,0:T(8,128)(2,1)}, bf16[2,512,128]{2,1,0:T(8,128)(2,1)S(1)}, u32[]{:S(2)}, u32[]{:S(2)}) %collective-permute-start.1) | collective-permute-done | bytes 262176 | tf_op jit(solution)/shard_map/ppermute | solution.py:28
  15.5 2.3 collective-permute-start.4
  18.5 2.7 collective-permute-start.6
  21.1 1.9 collective-permute-done.6.rest_11_
  26.5 128.9 %shard_map.56 = bf16[4,1024,512]{2,1,0:T(8,128)(2,1)} custom-call(s32[2]{0:T(128)} %pad_add_fusion.place, bf16[1024,4096]{1,0:T(8,128)(2,1)} %w_ref.9), custom_call_target="tpu_custom_call" | custom-call | bytes 8388608 | tf_op jit(solution)/shard_map/pallas_call | solution.py:220
  155.4 4.5 %collective-permute-start.29 = (bf16[4,1024,512]{2,1,0:T(8,128)(2,1)}, bf16[4,1024,512]{2,1,0:T(8,128)(2,1)}, u32[]{:S(2)}, u32[]{:S(2)}) collective-permute-start(bf16[4,1024,512]{2,1,0:T(8,128)(2,1)} %shard_map.56), channel_id=1, source_target_pairs={{0,1},{1,0},{2,3},{3,2},{4,5},{5,4},{6,7},{7,6},{8,9},{9,8},{10,11... | collective-permute-start | bytes 12582920 | tf_op jit(solution)/shard_map/ppermute | solution.py:37
  163.8 2.0 collective-permute-start.10
  166.9 3.0 collective-permute-start.12
  169.9 9.2 %collective-permute-done.13.rest_14_ = bf16[3,512,128]{2,1,0:T(8,128)(2,1)S(1)} collective-permute-done((bf16[3,512,128]{2,1,0:T(8,128)(2,1)S(1)}, bf16[3,512,128]{2,1,0:T(8,128)(2,1)S(1)}, u32[]{:S(2)}, u32[]{:S(2)}) %collective-permute-start.13) | collective-permute-done | bytes 393248 | tf_op jit(solution)/shard_map/ppermute | solution.py:28
  180.2 2.7 collective-permute-start.14
  184.0 2.7 collective-permute-start.18
  186.8 2.2 collective-permute-done.15.rest_8_
  191.4 2.5 collective-permute-done.17.rest_24_
  195.9 1.8 collective-permute-done.19.rest_16_
  199.2 2.7 collective-permute-start.22
  203.3 5.7 %collective-permute-done.23.rest_26_ = bf16[3,512,128]{2,1,0:T(8,128)(2,1)} collective-permute-done((bf16[3,512,128]{2,1,0:T(8,128)(2,1)}, bf16[3,512,128]{2,1,0:T(8,128)(2,1)}, u32[]{:S(2)}, u32[]{:S(2)}) %collective-permute-start.23) | collective-permute-done | bytes 393248 | tf_op jit(solution)/shard_map/ppermute | solution.py:28
  214.2 2.7 collective-permute-start.26
  217.7 1.9 collective-permute-start.24
  219.9 2.7 collective-permute-done.25.rest_20_
  234.1 17.9 %shard_map.55 = bf16[32,32,1024]{2,1,0:T(8,128)(2,1)S(1)} custom-call(s32[32]{0:T(128)S(1)} %fusion.codes, bf16[32,32,1024]{2,1,0:T(8,128)(2,1)S(1)} %copy-done.1, bf16[2,32,32,128]{3,2,1,0:T(8,128)(2,1)S(1)} %copy-done.10, bf16[2,512,128]{2,1,0:T(8,128)(2,1)S(1)} %bitcast.27, bf16[2,512,128]{2,1,0:T(8,128)(2,1)S(1)} %copy-done.7, ...), custom_call_target="tpu_custom_call" | custom-call | flops 2147483648 | bytes 16777216 | tf_op jit(solution)/shard_map/pallas_call | solution.py:183
  251.9 6.7 %collective-permute-start.28 = (bf16[1024,1024]{1,0:T(8,128)(2,1)S(1)}, bf16[1024,1024]{1,0:T(8,128)(2,1)S(1)}, u32[]{:S(2)}, u32[]{:S(2)}) collective-permute-start(bf16[1024,1024]{1,0:T(8,128)(2,1)S(1)} %bitcast.18), channel_id=1, source_target_pairs={{0,1},{1,0},{2,3},{3,2},{4,5},{5,4},{6,7},{7,6},{8,9},{9,8},{10,11... | collective-permute-start | bytes 6291464 | tf_op jit(solution)/shard_map/ppermute | solution.py:37
  258.7 3.8 %collective-permute-done.28.b_ref = bf16[1024,1024]{1,0:T(8,128)(2,1)S(1)} collective-permute-done((bf16[1024,1024]{1,0:T(8,128)(2,1)S(1)}, bf16[1024,1024]{1,0:T(8,128)(2,1)S(1)}, u32[]{:S(2)}, u32[]{:S(2)}) %collective-permute-start.28) | collective-permute-done | bytes 2097184 | tf_op jit(solution)/shard_map/ppermute | solution.py:37
  262.5 3.4 %copy-done = bf16[1024,4096]{1,0:T(8,128)(2,1)S(1)} copy-done((bf16[1024,4096]{1,0:T(8,128)(2,1)S(1)}, bf16[1024,4096]{1,0:T(8,128)(2,1)}, u32[]{:S(2)}) %copy-start) | copy-done | bytes 8388632
  265.9 4.9 %shard_map.59 = (bf16[512,512]{1,0:T(8,128)(2,1)S(1)}, bf16[512,512]{1,0:T(8,128)(2,1)S(1)}) custom-call(s32[2]{0:T(128)S(1)} %copy-done.24, bf16[1024,1024]{1,0:T(8,128)(2,1)S(1)} %bitcast.19, bf16[1024,1024]{1,0:T(8,128)(2,1)S(1)} %collective-permute-done.28.b_ref, bf16[1024,4096]{1,0:T(8,128)(2,1)S(1)} %copy-done, ...), custom_call_target="tpu_custom_call" | custom-call | flops 2147483648 | bytes 6291456 | tf_op jit(solution)/shard_map/pallas_call | solution.py:262
  273.7 5.6 %shard_map.60 = (bf16[512,512]{1,0:T(8,128)(2,1)S(1)}, bf16[512,512]{1,0:T(8,128)(2,1)S(1)}) custom-call(s32[2]{0:T(128)S(1)} %copy-done.24, bf16[1024,1024]{1,0:T(8,128)(2,1)S(1)} %bitcast.20, bf16[1024,1024]{1,0:T(8,128)(2,1)S(1)} %collective-permute-done.28.b_ref, bf16[1024,4096]{1,0:T(8,128)(2,1)S(1)} %copy-done, ...), custom_call_target="tpu_custom_call" | custom-call | flops 2147483648 | bytes 6291456 | tf_op jit(solution)/shard_map/pallas_call | solution.py:262
  280.8 5.6 %shard_map.58 = (bf16[512,512]{1,0:T(8,128)(2,1)S(1)}, bf16[512,512]{1,0:T(8,128)(2,1)S(1)}) custom-call(s32[2]{0:T(128)S(1)} %copy-done.24, bf16[1024,1024]{1,0:T(8,128)(2,1)S(1)} %bitcast.21, bf16[1024,1024]{1,0:T(8,128)(2,1)S(1)} %collective-permute-done.28.b_ref, bf16[1024,4096]{1,0:T(8,128)(2,1)S(1)} %copy-done, ...), custom_call_target="tpu_custom_call" | custom-call | flops 2147483648 | bytes 6291456 | tf_op jit(solution)/shard_map/pallas_call | solution.py:262
  286.8 2.7 collective-permute-start.35
  289.5 4.9 %shard_map.57.own = bf16[1024,512]{1,0:T(8,128)(2,1)S(1)} custom-call(s32[2]{0:T(128)S(1)} %copy-done.24, bf16[1024,1024]{1,0:T(8,128)(2,1)S(1)} %bitcast.22, bf16[1024,1024]{1,0:T(8,128)(2,1)S(1)} %collective-permute-done.28.b_ref, bf16[1024,4096]{1,0:T(8,128)(2,1)S(1)} %copy-done, bf16[4,1024,512]{2,1,0:T(8,128)(2,1)} %collective-permute-done.29.m_ref), custom_call_target="tpu_custom_call" | custom-call | flops 2147483648 | bytes 6291456 | tf_op jit(solution)/shard_map/pallas_call | solution.py:262
  296.6 11.2 %collective-permute-done.31.top1 = bf16[512,512]{1,0:T(8,128)(2,1)S(1)} collective-permute-done((bf16[512,512]{1,0:T(8,128)(2,1)S(1)}, bf16[512,512]{1,0:T(8,128)(2,1)S(1)}, u32[]{:S(2)}, u32[]{:S(2)}) %collective-permute-start.31) | collective-permute-done | bytes 524320 | tf_op jit(solution)/shard_map/ppermute | solution.py:33
  (122 shorter events, 46.8 us)
Async XLA Ops:
  0.0 9.1 %collective-permute-start.3 = (bf16[2,512,128]{2,1,0:T(8,128)(2,1)}, bf16[2,512,128]{2,1,0:T(8,128)(2,1)S(1)}, u32[]{:S(2)}, u32[]{:S(2)}) collective-permute-start(bf16[2,512,128]{2,1,0:T(8,128)(2,1)} %bitcast.23), channel_id=1, source_target_pairs={{0,64},{8,72},{16,80},{24,88},{32,96},{40,104},{48,112},{56,120},{... | collective-permute-start | bytes 786440 | tf_op jit(solution)/shard_map/ppermute | solution.py:28
  2.0 7.1 %collective-permute-start.2 = (bf16[2,512,128]{2,1,0:T(8,128)(2,1)}, bf16[2,512,128]{2,1,0:T(8,128)(2,1)S(1)}, u32[]{:S(2)}, u32[]{:S(2)}) collective-permute-start(bf16[2,512,128]{2,1,0:T(8,128)(2,1)} %bitcast.24), channel_id=1, source_target_pairs={{0,192},{8,200},{16,208},{24,216},{32,224},{40,232},{48,240},{56,2... | collective-permute-start | bytes 786440 | tf_op jit(solution)/shard_map/ppermute | solution.py:28
  3.3 11.4 %collective-permute-start.1 = (bf16[2,512,128]{2,1,0:T(8,128)(2,1)}, bf16[2,512,128]{2,1,0:T(8,128)(2,1)S(1)}, u32[]{:S(2)}, u32[]{:S(2)}) collective-permute-start(bf16[2,512,128]{2,1,0:T(8,128)(2,1)} %bitcast.25), channel_id=1, source_target_pairs={{0,8},{8,16},{16,24},{24,32},{32,40},{40,48},{48,56},{56,0},{64,72... | collective-permute-start | bytes 786440 | tf_op jit(solution)/shard_map/ppermute | solution.py:28
  5.1 9.6 %collective-permute-start = (bf16[2,512,128]{2,1,0:T(8,128)(2,1)}, bf16[2,512,128]{2,1,0:T(8,128)(2,1)S(1)}, u32[]{:S(2)}, u32[]{:S(2)}) collective-permute-start(bf16[2,512,128]{2,1,0:T(8,128)(2,1)} %bitcast.26), channel_id=1, source_target_pairs={{0,56},{8,0},{16,8},{24,16},{32,24},{40,32},{48,40},{56,48},{64,12... | collective-permute-start | bytes 786440 | tf_op jit(solution)/shard_map/ppermute | solution.py:28
  15.5 5.7 %collective-permute-start.7 = (bf16[1,512,128]{2,1,0:T(8,128)(2,1)S(1)}, bf16[1,512,128]{2,1,0:T(8,128)(2,1)S(1)}, u32[]{:S(2)}, u32[]{:S(2)}) collective-permute-start(bf16[1,512,128]{2,1,0:T(8,128)(2,1)S(1)} %slice.51), channel_id=1, source_target_pairs={{0,64},{8,72},{16,80},{24,88},{32,96},{40,104},{48,112},{56,120},{... | collective-permute-start | bytes 393224 | tf_op jit(solution)/shard_map/ppermute | solution.py:28
  15.5 7.6 %collective-permute-start.4 = (bf16[2,512,128]{2,1,0:T(8,128)(2,1)S(1)}, bf16[2,512,128]{2,1,0:T(8,128)(2,1)}, u32[]{:S(2)}, u32[]{:S(2)}) collective-permute-start(bf16[2,512,128]{2,1,0:T(8,128)(2,1)S(1)} %collective-permute-done.rest_1_), channel_id=1, source_target_pairs={{0,56},{8,0},{16,8},{24,16},{32,24},{40,32},{48,40},{56,48},{64,12... | collective-permute-start | bytes 786440 | tf_op jit(solution)/shard_map/ppermute | solution.py:28
  17.8 6.5 %collective-permute-start.5 = (bf16[2,512,128]{2,1,0:T(8,128)(2,1)S(1)}, bf16[2,512,128]{2,1,0:T(8,128)(2,1)}, u32[]{:S(2)}, u32[]{:S(2)}) collective-permute-start(bf16[2,512,128]{2,1,0:T(8,128)(2,1)S(1)} %collective-permute-done.1.rest_2_), channel_id=1, source_target_pairs={{0,8},{8,16},{16,24},{24,32},{32,40},{40,48},{48,56},{56,0},{64,72... | collective-permute-start | bytes 786440 | tf_op jit(solution)/shard_map/ppermute | solution.py:28
  24.3 142.5 %collective-permute-start.8 = (bf16[2,512,128]{2,1,0:T(8,128)(2,1)}, bf16[2,512,128]{2,1,0:T(8,128)(2,1)}, u32[]{:S(2)}, u32[]{:S(2)}) collective-permute-start(bf16[2,512,128]{2,1,0:T(8,128)(2,1)} %collective-permute-done.4.rest_3_), channel_id=1, source_target_pairs={{0,56},{8,0},{16,8},{24,16},{32,24},{40,32},{48,40},{56,48},{64,12... | collective-permute-start | bytes 786440 | tf_op jit(solution)/shard_map/ppermute | solution.py:28
  25.8 141.1 %collective-permute-start.9 = (bf16[2,512,128]{2,1,0:T(8,128)(2,1)}, bf16[2,512,128]{2,1,0:T(8,128)(2,1)}, u32[]{:S(2)}, u32[]{:S(2)}) collective-permute-start(bf16[2,512,128]{2,1,0:T(8,128)(2,1)} %collective-permute-done.5.rest_4_), channel_id=1, source_target_pairs={{0,8},{8,16},{16,24},{24,32},{32,40},{40,48},{48,56},{56,0},{64,72... | collective-permute-start | bytes 786440 | tf_op jit(solution)/shard_map/ppermute | solution.py:28
  155.4 107.1 %collective-permute-start.29 = (bf16[4,1024,512]{2,1,0:T(8,128)(2,1)}, bf16[4,1024,512]{2,1,0:T(8,128)(2,1)}, u32[]{:S(2)}, u32[]{:S(2)}) collective-permute-start(bf16[4,1024,512]{2,1,0:T(8,128)(2,1)} %shard_map.56), channel_id=1, source_target_pairs={{0,1},{1,0},{2,3},{3,2},{4,5},{5,4},{6,7},{7,6},{8,9},{9,8},{10,11... | collective-permute-start | bytes 12582920 | tf_op jit(solution)/shard_map/ppermute | solution.py:37
  162.5 16.6 %collective-permute-start.11 = (bf16[4,512,128]{2,1,0:T(8,128)(2,1)S(1)}, bf16[4,512,128]{2,1,0:T(8,128)(2,1)S(1)}, u32[]{:S(2)}, u32[]{:S(2)}) collective-permute-start(bf16[4,512,128]{2,1,0:T(8,128)(2,1)S(1)} %pad_maximum_fusion), channel_id=1, source_target_pairs={{0,64},{8,72},{16,80},{24,88},{32,96},{40,104},{48,112},{56,120},{... | collective-permute-start | bytes 1572872 | tf_op jit(solution)/shard_map/ppermute | solution.py:28
  163.8 15.4 %collective-permute-start.10 = (bf16[4,512,128]{2,1,0:T(8,128)(2,1)S(1)}, bf16[4,512,128]{2,1,0:T(8,128)(2,1)S(1)}, u32[]{:S(2)}, u32[]{:S(2)}) collective-permute-start(bf16[4,512,128]{2,1,0:T(8,128)(2,1)S(1)} %pad_maximum_fusion), channel_id=1, source_target_pairs={{0,192},{8,200},{16,208},{24,216},{32,224},{40,232},{48,240},{56,2... | collective-permute-start | bytes 1572872 | tf_op jit(solution)/shard_map/ppermute | solution.py:28
  166.8 12.3 %collective-permute-start.13 = (bf16[3,512,128]{2,1,0:T(8,128)(2,1)S(1)}, bf16[3,512,128]{2,1,0:T(8,128)(2,1)S(1)}, u32[]{:S(2)}, u32[]{:S(2)}) collective-permute-start(bf16[3,512,128]{2,1,0:T(8,128)(2,1)S(1)} %pad_maximum_fusion.1), channel_id=1, source_target_pairs={{0,8},{8,16},{16,24},{24,32},{32,40},{40,48},{48,56},{56,0},{64,72... | collective-permute-start | bytes 1179656 | tf_op jit(solution)/shard_map/ppermute | solution.py:28
  166.9 12.2 %collective-permute-start.12 = (bf16[3,512,128]{2,1,0:T(8,128)(2,1)S(1)}, bf16[3,512,128]{2,1,0:T(8,128)(2,1)S(1)}, u32[]{:S(2)}, u32[]{:S(2)}) collective-permute-start(bf16[3,512,128]{2,1,0:T(8,128)(2,1)S(1)} %pad_maximum_fusion.1), channel_id=1, source_target_pairs={{0,56},{8,0},{16,8},{24,16},{32,24},{40,32},{48,40},{56,48},{64,12... | collective-permute-start | bytes 1179656 | tf_op jit(solution)/shard_map/ppermute | solution.py:28
  180.2 6.5 %collective-permute-start.14 = (bf16[1,512,128]{2,1,0:T(8,128)(2,1)S(1)}, bf16[1,512,128]{2,1,0:T(8,128)(2,1)S(1)}, u32[]{:S(2)}, u32[]{:S(2)}) collective-permute-start(bf16[1,512,128]{2,1,0:T(8,128)(2,1)S(1)} %slice.57), channel_id=1, source_target_pairs={{0,56},{8,0},{16,8},{24,16},{32,24},{40,32},{48,40},{56,48},{64,12... | collective-permute-start | bytes 393224 | tf_op jit(solution)/shard_map/ppermute | solution.py:28
  184.0 12.0 %collective-permute-start.18 = (bf16[3,512,128]{2,1,0:T(8,128)(2,1)S(1)}, bf16[3,512,128]{2,1,0:T(8,128)(2,1)}, u32[]{:S(2)}, u32[]{:S(2)}) collective-permute-start(bf16[3,512,128]{2,1,0:T(8,128)(2,1)S(1)} %collective-permute-done.12.rest_13_), channel_id=1, source_target_pairs={{0,56},{8,0},{16,8},{24,16},{32,24},{40,32},{48,40},{56,48},{64,12... | collective-permute-start | bytes 1179656 | tf_op jit(solution)/shard_map/ppermute | solution.py:28
  186.6 11.1 %collective-permute-start.19 = (bf16[3,512,128]{2,1,0:T(8,128)(2,1)S(1)}, bf16[3,512,128]{2,1,0:T(8,128)(2,1)}, u32[]{:S(2)}, u32[]{:S(2)}) collective-permute-start(bf16[3,512,128]{2,1,0:T(8,128)(2,1)S(1)} %collective-permute-done.13.rest_14_), channel_id=1, source_target_pairs={{0,8},{8,16},{16,24},{24,32},{32,40},{40,48},{48,56},{56,0},{64,72... | collective-permute-start | bytes 1179656 | tf_op jit(solution)/shard_map/ppermute | solution.py:28
  186.7 7.2 %collective-permute-start.17 = (bf16[2,512,128]{2,1,0:T(8,128)(2,1)S(1)}, bf16[2,512,128]{2,1,0:T(8,128)(2,1)S(1)}, u32[]{:S(2)}, u32[]{:S(2)}) collective-permute-start(bf16[2,512,128]{2,1,0:T(8,128)(2,1)S(1)} %slice.60), channel_id=1, source_target_pairs={{0,64},{8,72},{16,80},{24,88},{32,96},{40,104},{48,112},{56,120},{... | collective-permute-start | bytes 786440 | tf_op jit(solution)/shard_map/ppermute | solution.py:28
  199.2 9.8 %collective-permute-start.23 = (bf16[3,512,128]{2,1,0:T(8,128)(2,1)}, bf16[3,512,128]{2,1,0:T(8,128)(2,1)}, u32[]{:S(2)}, u32[]{:S(2)}) collective-permute-start(bf16[3,512,128]{2,1,0:T(8,128)(2,1)} %pad_maximum_fusion.2), channel_id=1, source_target_pairs={{0,64},{8,72},{16,80},{24,88},{32,96},{40,104},{48,112},{56,120},{... | collective-permute-start | bytes 1179656 | tf_op jit(solution)/shard_map/ppermute | solution.py:28
  199.2 9.8 %collective-permute-start.22 = (bf16[3,512,128]{2,1,0:T(8,128)(2,1)}, bf16[3,512,128]{2,1,0:T(8,128)(2,1)}, u32[]{:S(2)}, u32[]{:S(2)}) collective-permute-start(bf16[3,512,128]{2,1,0:T(8,128)(2,1)} %pad_maximum_fusion.2), channel_id=1, source_target_pairs={{0,192},{8,200},{16,208},{24,216},{32,224},{40,232},{48,240},{56,2... | collective-permute-start | bytes 1179656 | tf_op jit(solution)/shard_map/ppermute | solution.py:28
  201.9 8.1 %collective-permute-start.20 = (bf16[3,512,128]{2,1,0:T(8,128)(2,1)}, bf16[3,512,128]{2,1,0:T(8,128)(2,1)}, u32[]{:S(2)}, u32[]{:S(2)}) collective-permute-start(bf16[3,512,128]{2,1,0:T(8,128)(2,1)} %collective-permute-done.18.rest_15_), channel_id=1, source_target_pairs={{0,56},{8,0},{16,8},{24,16},{32,24},{40,32},{48,40},{56,48},{64,12... | collective-permute-start | bytes 1179656 | tf_op jit(solution)/shard_map/ppermute | solution.py:28
  201.9 8.4 %collective-permute-start.21 = (bf16[3,512,128]{2,1,0:T(8,128)(2,1)}, bf16[3,512,128]{2,1,0:T(8,128)(2,1)}, u32[]{:S(2)}, u32[]{:S(2)}) collective-permute-start(bf16[3,512,128]{2,1,0:T(8,128)(2,1)} %collective-permute-done.19.rest_16_), channel_id=1, source_target_pairs={{0,8},{8,16},{16,24},{24,32},{32,40},{40,48},{48,56},{56,0},{64,72... | collective-permute-start | bytes 1179656 | tf_op jit(solution)/shard_map/ppermute | solution.py:28
  214.1 5.8 %collective-permute-start.27 = (bf16[3,256,128]{2,1,0:T(8,128)(2,1)S(1)}, bf16[3,256,128]{2,1,0:T(8,128)(2,1)S(1)}, u32[]{:S(2)}, u32[]{:S(2)}) collective-permute-start(bf16[3,256,128]{2,1,0:T(8,128)(2,1)S(1)} %slice.65), channel_id=1, source_target_pairs={{0,64},{8,72},{16,80},{24,88},{32,96},{40,104},{48,112},{56,120},{... | collective-permute-start | bytes 589832 | tf_op jit(solution)/shard_map/ppermute | solution.py:28
  214.2 5.7 %collective-permute-start.26 = (bf16[3,256,128]{2,1,0:T(8,128)(2,1)S(1)}, bf16[3,256,128]{2,1,0:T(8,128)(2,1)S(1)}, u32[]{:S(2)}, u32[]{:S(2)}) collective-permute-start(bf16[3,256,128]{2,1,0:T(8,128)(2,1)S(1)} %slice.64), channel_id=1, source_target_pairs={{0,192},{8,200},{16,208},{24,216},{32,224},{40,232},{48,240},{56,2... | collective-permute-start | bytes 589832 | tf_op jit(solution)/shard_map/ppermute | solution.py:28
  216.9 5.7 %collective-permute-start.25 = (bf16[3,256,128]{2,1,0:T(8,128)(2,1)S(1)}, bf16[3,256,128]{2,1,0:T(8,128)(2,1)S(1)}, u32[]{:S(2)}, u32[]{:S(2)}) collective-permute-start(bf16[3,256,128]{2,1,0:T(8,128)(2,1)S(1)} %slice.63), channel_id=1, source_target_pairs={{0,8},{8,16},{16,24},{24,32},{32,40},{40,48},{48,56},{56,0},{64,72... | collective-permute-start | bytes 589832 | tf_op jit(solution)/shard_map/ppermute | solution.py:28
  251.9 10.5 %collective-permute-start.28 = (bf16[1024,1024]{1,0:T(8,128)(2,1)S(1)}, bf16[1024,1024]{1,0:T(8,128)(2,1)S(1)}, u32[]{:S(2)}, u32[]{:S(2)}) collective-permute-start(bf16[1024,1024]{1,0:T(8,128)(2,1)S(1)} %bitcast.18), channel_id=1, source_target_pairs={{0,1},{1,0},{2,3},{3,2},{4,5},{5,4},{6,7},{7,6},{8,9},{9,8},{10,11... | collective-permute-start | bytes 6291464 | tf_op jit(solution)/shard_map/ppermute | solution.py:37
  270.8 15.6 %collective-permute-start.30 = (bf16[512,512]{1,0:T(8,128)(2,1)S(1)}, bf16[512,512]{1,0:T(8,128)(2,1)S(1)}, u32[]{:S(2)}, u32[]{:S(2)}) collective-permute-start(bf16[512,512]{1,0:T(8,128)(2,1)S(1)} %get-tuple-element.60), channel_id=1, source_target_pairs={{0,2},{1,3},{2,4},{3,5},{4,6},{5,7},{6,0},{7,1},{8,10},{9,11},{10,... | collective-permute-start | bytes 1572872 | tf_op jit(solution)/shard_map/ppermute | solution.py:33
  272.2 14.4 %collective-permute-start.34 = (bf16[512,512]{1,0:T(8,128)(2,1)S(1)}, bf16[512,512]{1,0:T(8,128)(2,1)S(1)}, u32[]{:S(2)}, u32[]{:S(2)}) collective-permute-start(bf16[512,512]{1,0:T(8,128)(2,1)S(1)} %get-tuple-element.64), channel_id=1, source_target_pairs={{0,6},{1,7},{2,0},{3,1},{4,2},{5,3},{6,4},{7,5},{8,14},{9,15},{10,... | collective-permute-start | bytes 1572872 | tf_op jit(solution)/shard_map/ppermute | solution.py:33
  279.3 17.0 %collective-permute-start.32 = (bf16[512,512]{1,0:T(8,128)(2,1)S(1)}, bf16[512,512]{1,0:T(8,128)(2,1)S(1)}, u32[]{:S(2)}, u32[]{:S(2)}) collective-permute-start(bf16[512,512]{1,0:T(8,128)(2,1)S(1)} %get-tuple-element.61), channel_id=1, source_target_pairs={{0,6},{1,7},{2,0},{3,1},{4,2},{5,3},{6,4},{7,5},{8,14},{9,15},{10,... | collective-permute-start | bytes 1572872 | tf_op jit(solution)/shard_map/ppermute | solution.py:33
  280.7 15.9 %collective-permute-start.33 = (bf16[512,512]{1,0:T(8,128)(2,1)S(1)}, bf16[512,512]{1,0:T(8,128)(2,1)S(1)}, u32[]{:S(2)}, u32[]{:S(2)}) collective-permute-start(bf16[512,512]{1,0:T(8,128)(2,1)S(1)} %get-tuple-element.62), channel_id=1, source_target_pairs={{0,2},{1,3},{2,4},{3,5},{4,6},{5,7},{6,0},{7,1},{8,10},{9,11},{10,... | collective-permute-start | bytes 1572872 | tf_op jit(solution)/shard_map/ppermute | solution.py:33
  286.6 21.3 %collective-permute-start.31 = (bf16[512,512]{1,0:T(8,128)(2,1)S(1)}, bf16[512,512]{1,0:T(8,128)(2,1)S(1)}, u32[]{:S(2)}, u32[]{:S(2)}) collective-permute-start(bf16[512,512]{1,0:T(8,128)(2,1)S(1)} %add_convert_fusion.1), channel_id=1, source_target_pairs={{0,2},{1,3},{2,4},{3,5},{4,6},{5,7},{6,0},{7,1},{8,10},{9,11},{10,... | collective-permute-start | bytes 1572872 | tf_op jit(solution)/shard_map/ppermute | solution.py:33
  286.8 21.1 %collective-permute-start.35 = (bf16[512,512]{1,0:T(8,128)(2,1)S(1)}, bf16[512,512]{1,0:T(8,128)(2,1)S(1)}, u32[]{:S(2)}, u32[]{:S(2)}) collective-permute-start(bf16[512,512]{1,0:T(8,128)(2,1)S(1)} %add_convert_fusion), channel_id=1, source_target_pairs={{0,6},{1,7},{2,0},{3,1},{4,2},{5,3},{6,4},{7,5},{8,14},{9,15},{10,... | collective-permute-start | bytes 1572872 | tf_op jit(solution)/shard_map/ppermute | solution.py:33
  (31 other events, 528.2 us)
